TPU v7x, 32 devices: a whole 2x2x4 slice. The times are simulated.
32 devices in a mesh: seq: 16 (over z, y, x), vis: 2 (over core).
Axes of the slice: x: 2, y: 2, z: 4, core: 2. Of those that a mesh axis runs over, the one named last changes fastest.
Arguments:
- queries: bfloat16 [4096, 4096], P('seq', 'vis'), may hold values from -120 to 120
- keys: bfloat16 [64, 8, 512], P('seq', 'vis'), may hold values from -7 to 7
- values: bfloat16 [64, 8, 512], P('seq', 'vis'), may hold values from -6 to 6
- grad_out: bfloat16 [4096, 4096], P('seq', 'vis'), may hold values from -6 to 6
- block_map: int32 [16, 8], replicated, may hold values from 0 to 63, as said below
- block_count: int32 [16], replicated, may hold values from 6 to 8, as said below
Outputs:
- grad_queries: bfloat16 [4096, 4096], P('seq', 'vis')
- log_totals: float32 [32, 4096], P('vis', 'seq')
- grad_keys: bfloat16 [64, 8, 512], P('seq', 'vis')
- grad_values: bfloat16 [64, 8, 512], P('seq', 'vis')
Inputs may be any that keep to these rules, and one draw needn't show every extreme that they name: `block_map`: block b belongs to seq index b // 4; the 8 blocks that one span names belong to 8 different seq indices. `block_count`: some span attends all 8 of its named blocks.
All inputs are finite; a program needn't handle non-finite values.
Results may differ from a plain program's by a relative error of at most 0.014.
Values may be sent and summed in bfloat16 or wider, within the bound.
No kernel may reach another device: no remote copies, remote signals or barrier semaphores. Data moves between devices by JAX's collectives and lax.ppermute only.
A program may use at most 64 MiB of HBM per device.

v0:
```python
import math

import jax
import jax.numpy as jnp
from jax import lax
from jax.sharding import PartitionSpec as P

HEAD_DIM = 128
GROUP = 8


def contract_rows(left, right):
    return lax.dot_general(
        left, right, (((0,), (0,)), ((), ())), preferred_element_type=jnp.float32
    )


def contract_cols(left, right):
    return lax.dot_general(
        left, right, (((1,), (1,)), ((), ())), preferred_element_type=jnp.float32
    )


def add_columns(total, term, start):
    current = lax.dynamic_slice_in_dim(total, start, HEAD_DIM, 1)
    return lax.dynamic_update_slice_in_dim(total, current + term, start, 1)


def attend(queries, grad_out, key_rows, value_rows, key_live, first_head):
    score_scale = 1.0 / math.sqrt(HEAD_DIM)
    head_count = queries.shape[1] // HEAD_DIM
    query_parts, log_parts = ([], [])
    key_total = jnp.zeros(key_rows.shape, jnp.float32)
    value_total = jnp.zeros(value_rows.shape, jnp.float32)
    for head_index in range(head_count):
        low = head_index * HEAD_DIM
        high = low + HEAD_DIM
        kv_start = (first_head + head_index) // GROUP * HEAD_DIM
        q_head = queries[:, low:high]
        g_head = grad_out[:, low:high]
        k_head = lax.dynamic_slice_in_dim(key_rows, kv_start, HEAD_DIM, 1)
        v_head = lax.dynamic_slice_in_dim(value_rows, kv_start, HEAD_DIM, 1)
        scores = contract_cols(q_head, k_head) * score_scale
        scores = jnp.where(key_live[None, :], scores, -1e30)
        row_max = jnp.max(scores, axis=1)
        weights = jnp.exp(scores - row_max[:, None])
        totals = jnp.sum(weights, axis=1)
        probs_full = weights / totals[:, None]
        probs_low = probs_full.astype(jnp.bfloat16)
        context = jnp.dot(probs_low, v_head, preferred_element_type=jnp.float32)
        delta_row = jnp.sum(g_head.astype(jnp.float32) * context, axis=1)
        value_total = add_columns(value_total, contract_rows(probs_low, g_head), kv_start)
        grad_probs = contract_cols(g_head, v_head)
        grad_scores = (probs_full * (grad_probs - delta_row[:, None])).astype(jnp.bfloat16)
        query_parts.append(
            jnp.dot(grad_scores, k_head, preferred_element_type=jnp.float32) * score_scale
        )
        key_total = add_columns(
            key_total, contract_rows(grad_scores, q_head) * score_scale, kv_start
        )
        log_parts.append(row_max + jnp.log(totals))
    grad_query = jnp.concatenate(query_parts, axis=1).astype(jnp.bfloat16)
    return (grad_query, jnp.stack(log_parts, axis=0), key_total, value_total)


def local(queries, keys, values, grad_out, block_map, block_count):
    seq_count = lax.axis_size("seq")
    my_seq = lax.axis_index("seq")
    my_vis = lax.axis_index("vis")
    first_head = my_vis * (queries.shape[1] // HEAD_DIM)
    per_owner = keys.shape[0]
    most_blocks = block_map.shape[1]
    owner_seq = block_map // per_owner
    local_block = block_map % per_owner
    live_blocks = jnp.arange(most_blocks, dtype=jnp.int32)[None, :] < block_count[:, None]
    asked_here = (owner_seq == my_seq) & live_blocks
    requested = jnp.any(asked_here, axis=1)
    local_slot = jnp.sum(jnp.where(asked_here, local_block, 0), axis=1)
    my_owners = lax.dynamic_index_in_dim(owner_seq, my_seq, 0, keepdims=False)
    my_count = lax.dynamic_index_in_dim(block_count, my_seq, 0, keepdims=False)
    my_live = jnp.arange(most_blocks, dtype=jnp.int32) < my_count
    source_ids = jnp.arange(seq_count, dtype=jnp.int32)
    from_source = jnp.any((my_owners[None, :] == source_ids[:, None]) & my_live[None, :], axis=1)
    stacked = jnp.stack([keys, values])
    whole_rows = lax.all_gather(stacked, "vis", axis=2, tiled=True)
    selected = whole_rows[:, local_slot]
    fetched = lax.all_to_all(
        jnp.where(requested[None, :, None, None], selected, jnp.zeros_like(selected)),
        "seq",
        split_axis=1,
        concat_axis=1,
        tiled=True,
    )
    block_rows = fetched.shape[2]
    col_width = fetched.shape[3]
    key_live = jnp.repeat(from_source, block_rows)
    key_value_rows = fetched.reshape(2, -1, col_width)
    grad_query, log_totals, key_terms, value_terms = attend(
        queries, grad_out, key_value_rows[0], key_value_rows[1], key_live, first_head
    )
    partial_terms = jnp.stack([key_terms, value_terms]).reshape(2, -1, block_rows, col_width)
    owner_onehot = (
        requested[None, :]
        & (local_slot[None, :] == jnp.arange(per_owner, dtype=jnp.int32)[:, None])
    ).astype(jnp.float32)
    returned = lax.all_to_all(
        partial_terms.astype(jnp.bfloat16), "seq", split_axis=1, concat_axis=1, tiled=True
    ).astype(partial_terms.dtype)
    returned_flat = returned.reshape(2, seq_count, -1)
    summed = jnp.einsum("ln,tnx->tlx", owner_onehot, returned_flat, precision=lax.Precision.HIGHEST)
    grad_blocks = lax.psum_scatter(
        summed.reshape(2, per_owner, returned.shape[2], returned.shape[3]).astype(jnp.bfloat16),
        "vis",
        scatter_dimension=2,
        tiled=True,
    ).astype(jnp.float32)
    grad_blocks = grad_blocks.astype(jnp.bfloat16)
    return (grad_query, log_totals, grad_blocks[0], grad_blocks[1])


def solution(mesh):
    in_specs = (
        P("seq", "vis"),
        P("seq", "vis", None),
        P("seq", "vis", None),
        P("seq", "vis"),
        P(),
        P(),
    )
    out_specs = (P("seq", "vis"), P("vis", "seq"), P("seq", "vis", None), P("seq", "vis", None))
    return jax.shard_map(local, mesh=mesh, in_specs=in_specs, out_specs=out_specs, check_vma=False)
```

profile of v0, /device:TPU:0, one launch (start us, length us, event | category | flops | bytes accessed | tf_op | source)
XLA Modules:
  0.0 94.3 jit_solution(14937848979481232636)
XLA Ops:
  7.2 0.7 copy-done.8
  7.9 0.7 fusion.432
  8.6 0.7 copy_bitcast_fusion
  9.4 2.0 %all_gather.3 = bf16[2,4,8,512]{3,1,0,2:T(4,128)(2,1)S(1)} all-gather(bf16[2,4,4,512]{3,1,0,2:T(4,128)(2,1)S(1)} %pad_maximum_fusion), channel_id=1, replica_groups=mesh['seq'=16,'vis'=2] {'vis'}, dimensions={2}, use_global_device_ids=true | all-gather | bytes 98304 | tf_op jit(solution)/shard_map/all_gather | solution.py:85
  11.4 0.6 gather_fusion
  11.9 0.8 select_bitcast_fusion
  12.7 8.2 %all-to-all-start = ((bf16[2,16,8,512]{3,2,0,1:T(8,128)(2,1)}), bf16[2,16,8,512]{3,2,0,1:T(8,128)(2,1)S(1)}, u32[]{:S(2)}, u32[]{:S(2)}) async-start(bf16[2,16,8,512]{3,2,0,1:T(8,128)(2,1)} %select_bitcast_fusion), calls=%async_computation | async-start | bytes 524288 | tf_op jit(solution)/shard_map/all_to_all | solution.py:87
  21.1 0.6 copy-done.10
  21.7 0.6 dynamic_slice.195
  22.5 0.7 iota_compare_fusion.3
  23.4 0.3 fusion.434
  23.7 0.7 copy.127
  24.4 0.7 copy.126
  25.1 0.7 copy.125
  25.9 0.7 copy.124
  26.6 0.7 copy.123
  27.3 0.7 copy.122
  29.3 0.6 copy-done.11
  30.0 0.6 dynamic-slice
  38.2 0.8 copy-done.7
  39.0 0.2 fusion.96
  39.4 0.7 copy-done.6
  40.1 0.2 fusion.95
  40.5 0.7 copy-done.5
  41.2 0.2 fusion.94
  41.6 0.6 copy-done.4
  42.2 0.2 fusion.93
  42.7 0.6 copy-done.3
  43.3 0.2 fusion.92
  43.7 0.6 copy-done.2
  44.4 0.2 fusion.91
  44.8 0.2 fusion.90
  45.2 0.2 fusion.89
  45.7 0.2 fusion.88
  46.1 0.2 fusion.87
  46.5 0.2 fusion.86
  46.9 0.2 fusion.85
  47.4 0.2 fusion.84
  47.8 0.2 fusion.83
  48.2 0.2 fusion.82
  48.6 0.2 fusion.81
  49.1 0.2 fusion.50
  51.9 0.7 copy.106
  52.7 6.8 %all-to-all-start.1 = ((bf16[2,16,8,512]{3,2,0,1:T(8,128)(2,1)}), bf16[2,16,8,512]{3,2,0,1:T(8,128)(2,1)S(1)}, u32[]{:S(2)}, u32[]{:S(2)}) async-start(bf16[2,16,8,512]{3,2,0,1:T(8,128)(2,1)} %copy.106), calls=%async_computation.1 | async-start | bytes 524288 | tf_op jit(solution)/shard_map/all_to_all | solution.py:106
  59.5 0.2 fusion.52
  59.8 0.2 fusion.54
  60.0 0.2 fusion.56
  60.4 0.2 fusion.60
  60.7 0.2 fusion.62
  60.9 0.2 fusion.64
  61.3 0.2 fusion.68
  61.6 0.2 fusion.70
  61.8 0.2 fusion.72
  62.0 0.2 fusion.74
  62.2 0.2 fusion.76
  62.5 0.2 fusion.78
  62.7 0.2 fusion.80
  62.9 6.2 %all-to-all-done.1 = bf16[2,16,8,512]{3,2,0,1:T(8,128)(2,1)S(1)} async-done(((bf16[2,16,8,512]{3,2,0,1:T(8,128)(2,1)}), bf16[2,16,8,512]{3,2,0,1:T(8,128)(2,1)S(1)}, u32[]{:S(2)}, u32[]{:S(2)}) %all-to-all-start.1) | async-done | bytes 262176 | tf_op jit(solution)/shard_map/all_to_all | solution.py:106
  69.3 0.3 fusion
  69.6 0.7 convert_element_type.213
  70.3 1.4 %copy.108 = bf16[256,2048]{1,0:T(8,128)(2,1)} copy(bf16[256,2048]{0,1:T(8,128)(2,1)S(1)} %fusion.80) | data formatting | bytes 2097152
  71.7 1.2 %stack.22 = f32[16,256]{1,0:T(8,128)} concatenate(f32[1,256]{1,0:T(1,128)S(1)} %bitcast.108, f32[1,256]{1,0:T(1,128)S(1)} %bitcast.107, f32[1,256]{1,0:T(1,128)S(1)} %bitcast.106, f32[1,256]{1,0:T(1,128)S(1)} %bitcast.105, f32[1,256]{1,0:T(1,128)S(1)} %bitcast.104, f32[1,256]{1,0:T(1,128)S(1)} %bitcast.103, f32[1,256]{1,0:T(1,128)S(1)} %bitcast.102, f32[1,256]{1,0:T(1,128)S(1)} %bitcast.101, ...), dimensions={0} | concatenate | bytes 32768 | tf_op jit(solution)/shard_map/stack | solution.py:63
  72.9 13.1 %all-reduce.3.cloned.1.call-done = bf16[2,4,8,512]{3,2,1,0:T(8,128)(2,1)} async-done(((bf16[2,4,8,512]{3,2,1,0:T(8,128)(2,1)}), bf16[2,4,8,512]{3,2,1,0:T(8,128)(2,1)}) %all-reduce.3.cloned.1.call-update) | async-done | bytes 65552
  86.0 1.4 %dynamic-slice_bitcast_fusion = (bf16[4,4,512]{2,1,0:T(4,128)(2,1)}, bf16[4,4,512]{2,1,0:T(4,128)(2,1)}) fusion(bf16[2,4,8,512]{3,2,1,0:T(8,128)(2,1)} %all-reduce.3.cloned.1.call-done, u32[]{:T(128)S(6)} %convert.73, u32[]{:T(128)S(6)} %multiply.1), kind=kLoop, calls=%fused_computation.474 | loop fusion | bytes 65544 | tf_op jit(solution)/shard_map/squeeze | solution.py:118
  (144 shorter events, 14.7 us)
Async XLA Ops:
  7.2 0.7 copy-start.8
  7.2 1.4 %copy-start.9 = (bf16[4,4,512]{2,1,0:T(4,128)(2,1)S(1)}, bf16[4,4,512]{2,1,0:T(4,128)(2,1)}, u32[]{:S(2)}) copy-start(bf16[4,4,512]{2,1,0:T(4,128)(2,1)} %param.8) | copy-start | bytes 49156
  11.3 12.0 %copy-start.1 = (bf16[256,2048]{1,0:T(8,128)(2,1)S(1)}, bf16[256,2048]{1,0:T(8,128)(2,1)}, u32[]{:S(2)}) copy-start(bf16[256,2048]{1,0:T(8,128)(2,1)} %param.9) | copy-start | bytes 3145732
  12.7 18.5 %all-to-all-start = ((bf16[2,16,8,512]{3,2,0,1:T(8,128)(2,1)}), bf16[2,16,8,512]{3,2,0,1:T(8,128)(2,1)S(1)}, u32[]{:S(2)}, u32[]{:S(2)}) async-start(bf16[2,16,8,512]{3,2,0,1:T(8,128)(2,1)} %select_bitcast_fusion), calls=%async_computation | async-start | bytes 524288 | tf_op jit(solution)/shard_map/all_to_all | solution.py:87
  21.0 0.7 copy-start.10
  27.3 3.9 %copy-start = (bf16[256,2048]{1,0:T(8,128)(2,1)S(1)}, bf16[256,2048]{1,0:T(8,128)(2,1)}, u32[]{:S(2)}) copy-start(bf16[256,2048]{1,0:T(8,128)(2,1)} %param.6) | copy-start | bytes 3145732
  29.3 0.7 copy-start.11
  38.2 0.8 copy-start.7
  39.2 0.8 copy-start.6
  40.3 0.8 copy-start.5
  41.4 0.8 copy-start.4
  42.5 0.8 copy-start.3
  43.6 0.8 copy-start.2
  52.7 16.4 %all-to-all-start.1 = ((bf16[2,16,8,512]{3,2,0,1:T(8,128)(2,1)}), bf16[2,16,8,512]{3,2,0,1:T(8,128)(2,1)S(1)}, u32[]{:S(2)}, u32[]{:S(2)}) async-start(bf16[2,16,8,512]{3,2,0,1:T(8,128)(2,1)} %copy.106), calls=%async_computation.1 | async-start | bytes 524288 | tf_op jit(solution)/shard_map/all_to_all | solution.py:106
  59.5 26.6 %all-reduce.3.cloned.1.call-start = ((), (), s32[]{:S(2)}) async-start(), calls=%async_computation.2 | async-start | bytes 131072
Sparse Core Ops, SparseCore 0:
  70.4 15.6 all-reduce.2
where the time goes:
time: 95.1 us; the launch traced here: 94.3 us
  local copies, waits for them, and re-layouts  20.3 us (21%)
  waiting for transfers between devices  19.3 us (20%)
  matrix products  18.8 us (20%)
  between operations  15.5 us (16%)
  starting transfers between devices  15 us (16%)
  other arithmetic  3.27 us (3%)
  blocking collectives  1.96 us (2%)
    unnamed x45, local copies, waits for them, and re-layouts  13.8 us
    unnamed x2, waiting for transfers between devices  13.1 us
    all_to_all x1, starting transfers between devices, local(): lax.all_to_all(jnp.where(requested[None, :, None, None], selected, jnp.ze...  8.21 us
    all_to_all x1, starting transfers between devices, local(): lax.all_to_all(partial_terms.astype(jnp.bfloat16), 'seq', split_axis=1, c...  6.8 us
    all_to_all x1, waiting for transfers between devices, local(): lax.all_to_all(partial_terms.astype(jnp.bfloat16), 'seq', split_axis=1, c...  6.2 us
    dot_general x32, matrix products, contract_cols(): lax.dot_general(left, right, (((1,), (1,)), ((), ())), preferred_element_...  6.14 us
    dot_general x32, matrix products, contract_rows(): lax.dot_general(left, right, (((0,), (0,)), ((), ())), preferred_element_...  5.13 us
    dot_general x16, matrix products, attend(): context = jnp.dot(probs_low, v_head, preferred_element_type=jnp.float32)  3.77 us
  transfers between devices with their start and end apart: 3, of which 2 were waited for; matrix products, arithmetic and copies ran while one was open for 15% of the time, Pallas kernels for 0%

commit v1 on v0

v1 whole, which is shorter than its diff:
```python
import functools
import math

import jax
import jax.numpy as jnp
from jax import lax
from jax.experimental import pallas as pl
from jax.experimental.pallas import tpu as pltpu
from jax.sharding import PartitionSpec as P

HEAD_DIM = 128
GROUP = 8
BF16 = jnp.bfloat16
F32 = jnp.float32
VMEM = pl.BlockSpec(memory_space=pltpu.VMEM)


def iota(shape, dim):
    return lax.broadcasted_iota(jnp.int32, shape, dim)


def dot(left, right, left_dim=1, right_dim=0):
    return lax.dot_general(
        left, right, (((left_dim,), (right_dim,)), ((), ())), preferred_element_type=F32
    )


def slot_of_span(block_map, block_count, me, per_owner):
    live = iota(block_map.shape, 1) < block_count
    asked = live & (block_map // per_owner == me)
    return jnp.sum(jnp.where(asked, block_map % per_owner + 1, 0), axis=1, keepdims=True) - 1


def route(slot, rows, per_owner, span_dim):
    spans = slot.shape[0]
    span_rows, slot_rows = spans * 2 * rows, 2 * per_owner * rows
    expand = (iota((span_rows, spans), 0) // (2 * rows) == iota((span_rows, spans), 1)).astype(BF16)
    if span_dim == 0:
        shape = (span_rows, slot_rows)
        want = dot(expand, jnp.broadcast_to(slot, (spans, slot_rows)).astype(BF16))
    else:
        shape = (slot_rows, span_rows)
        want = dot(jnp.broadcast_to(slot, (spans, slot_rows)).astype(BF16), expand, 0, 1)
    place = iota(shape, span_dim) % (2 * rows)
    have = iota(shape, 1 - span_dim)
    have_slot = have % (per_owner * rows) // rows
    have_place = have // (per_owner * rows) * rows + have % rows
    return ((want == have_slot.astype(F32)) & (place == have_place)).astype(BF16)


def send_kernel(width, starts, rows, per_owner, me_ref, map_ref, count_ref, keys_ref, values_ref, out_ref):
    slot = jnp.maximum(slot_of_span(map_ref[...], count_ref[...], me_ref[0], per_owner), 0)
    pick = route(slot, rows, per_owner, 0)
    stacked = jnp.concatenate([keys_ref[...], values_ref[...]], axis=0)
    for core, start in enumerate(starts):
        out_ref[core] = dot(pick, stacked[:, start : start + width]).astype(BF16)


def sum_kernel(width, starts, rows, per_owner, me_ref, map_ref, count_ref, terms_ref, keys_ref, values_ref):
    slot = slot_of_span(map_ref[...], count_ref[...], me_ref[0], per_owner)
    pick = route(slot, rows, per_owner, 1)
    half = per_owner * rows
    done = {}
    for core, start in enumerate(starts):
        part = dot(pick, terms_ref[core])
        done[start] = done[start] + part if start in done else part
    for start, total in done.items():
        keys_ref[:, start : start + width] = total[:half].astype(BF16)
        values_ref[:, start : start + width] = total[half:].astype(BF16)


def attend_kernel(
    rows, per_owner, cores, spans, me_ref, map_ref, count_ref, q_ref, g_ref, rows_ref, gq_ref, log_ref, terms_ref
):
    score_scale = 1.0 / math.sqrt(HEAD_DIM)
    me = me_ref[0]
    most = map_ref.shape[1]
    block_rows = cores * rows
    keys = most * block_rows
    kv_heads = rows_ref.shape[1] // HEAD_DIM
    heads = q_ref.shape[1] // HEAD_DIM
    tokens = q_ref.shape[0]
    per_kv = heads // kv_heads
    row = map_ref[pl.ds(me, 1), :]
    count = count_ref[pl.ds(me, 1), :]

    shape = (2 * keys, rows_ref.shape[0])
    mine, theirs = iota((2 * keys, 1), 0), iota(shape, 1)
    block = mine % keys // block_rows
    owner = jnp.sum(jnp.where(iota((2 * keys, most), 1) == block, row // per_owner, 0), axis=1, keepdims=True)
    place = ((mine % block_rows // rows * spans + owner) * 2 + mine // keys) * rows + mine % rows
    place = jnp.where(block < count, place, -1)
    pick = (place == theirs).astype(BF16)
    fetched = dot(pick, rows_ref[...]).astype(BF16)
    live = (iota((2, keys, tokens), 1) // block_rows) < count.reshape(1, 1, 1)

    gk_parts, gv_parts = [], []
    for kv in range(kv_heads):
        cols = slice(kv * HEAD_DIM, (kv + 1) * HEAD_DIM)
        k, v = fetched[:keys, cols], fetched[keys:, cols]
        zero = jnp.zeros_like(k)
        k2 = jnp.concatenate([jnp.concatenate([k, zero], 1), jnp.concatenate([zero, k], 1)], 0)
        v2 = jnp.concatenate([jnp.concatenate([v, zero], 1), jnp.concatenate([zero, v], 1)], 0)
        gk = jnp.zeros((2 * keys, 2 * HEAD_DIM), F32)
        gv = jnp.zeros((2 * keys, 2 * HEAD_DIM), F32)
        for pair in range(per_kv // 2):
            head = kv * per_kv + 2 * pair
            at = slice(head * HEAD_DIM, (head + 2) * HEAD_DIM)
            q, g = q_ref[:, at], g_ref[:, at]
            scores = (dot(k2, q, 1, 1) * score_scale).reshape(2, keys, tokens)
            scores = jnp.where(live, scores, -1e30)
            row_max = jnp.max(scores, axis=1, keepdims=True)
            weights = jnp.exp(scores - row_max)
            totals = jnp.sum(weights, axis=1, keepdims=True)
            probs = weights * (1.0 / totals)
            log_ref[head : head + 2, :] = (row_max + jnp.log(totals)).reshape(2, tokens)
            low = probs.astype(BF16)
            grad_probs = dot(v2, g, 1, 1).reshape(2, keys, tokens)
            delta = jnp.sum(low.astype(F32) * grad_probs, axis=1, keepdims=True)
            gs = (probs * (grad_probs - delta)).astype(BF16).reshape(2 * keys, tokens)
            gv += dot(low.reshape(2 * keys, tokens), g)
            gk += dot(gs, q)
            gq_ref[:, at] = (dot(gs, k2, 0, 0) * score_scale).astype(BF16)
        gk_parts.append((gk[:keys, :HEAD_DIM] + gk[keys:, HEAD_DIM:]) * score_scale)
        gv_parts.append(gv[:keys, :HEAD_DIM] + gv[keys:, HEAD_DIM:])
    terms = jnp.concatenate([jnp.concatenate(gk_parts, 1), jnp.concatenate(gv_parts, 1)], 0).astype(BF16)
    terms_ref[...] = dot(pick, terms, 0, 0).astype(BF16)


def local(queries, keys, values, grad_out, block_map, block_count):
    spans, cores = lax.axis_size("seq"), lax.axis_size("vis")
    me = lax.axis_index("seq").astype(jnp.int32).reshape(1)
    per_owner, rows, columns = keys.shape
    heads = queries.shape[1] // HEAD_DIM
    width = max(heads // GROUP, 1) * HEAD_DIM
    starts = tuple(core * heads // GROUP * HEAD_DIM for core in range(cores))
    tokens = queries.shape[0]
    counts = block_count.reshape(spans, 1)
    flat = (per_owner * rows, columns)
    smem = pl.BlockSpec(memory_space=pltpu.SMEM)
    params = pltpu.CompilerParams(vmem_limit_bytes=32 * 1024 * 1024)

    sent = pl.pallas_call(
        functools.partial(send_kernel, width, starts, rows, per_owner),
        out_shape=jax.ShapeDtypeStruct((cores, spans * 2 * rows, width), BF16),
        in_specs=[smem, VMEM, VMEM, VMEM, VMEM],
        out_specs=VMEM,
        compiler_params=params,
        name="choose_blocks",
    )(me, block_map, counts, keys.reshape(flat), values.reshape(flat))
    got = lax.all_to_all(
        sent.reshape(cores * spans, 2 * rows, width), ("vis", "seq"), split_axis=0, concat_axis=0, tiled=True
    )
    grad_queries, log_totals, terms = pl.pallas_call(
        functools.partial(attend_kernel, rows, per_owner, cores, spans),
        out_shape=(
            jax.ShapeDtypeStruct(queries.shape, BF16),
            jax.ShapeDtypeStruct((heads, tokens), F32),
            jax.ShapeDtypeStruct((cores * spans * 2 * rows, width), BF16),
        ),
        in_specs=[smem] + [VMEM] * 5,
        out_specs=(VMEM, VMEM, VMEM),
        compiler_params=params,
        name="attend",
    )(me, block_map, counts, queries, grad_out, got.reshape(-1, width))
    back = lax.all_to_all(
        terms.reshape(cores * spans, 2 * rows, width), ("vis", "seq"), split_axis=0, concat_axis=0, tiled=True
    )
    grad_keys, grad_values = pl.pallas_call(
        functools.partial(sum_kernel, width, starts, rows, per_owner),
        out_shape=(jax.ShapeDtypeStruct(flat, BF16),) * 2,
        in_specs=[smem, VMEM, VMEM, VMEM],
        out_specs=(VMEM, VMEM),
        compiler_params=params,
        name="sum_blocks",
    )(me, block_map, counts, back.reshape(cores, -1, width))
    return (grad_queries, log_totals, grad_keys.reshape(keys.shape), grad_values.reshape(keys.shape))


def solution(mesh):
    in_specs = (
        P("seq", "vis"),
        P("seq", "vis", None),
        P("seq", "vis", None),
        P("seq", "vis"),
        P(),
        P(),
    )
    out_specs = (P("seq", "vis"), P("vis", "seq"), P("seq", "vis", None), P("seq", "vis", None))
    return jax.shard_map(local, mesh=mesh, in_specs=in_specs, out_specs=out_specs, check_vma=False)
```

time: 95.1 us -> 36.6 us (0.38)
  blocking collectives: 1.96 us -> 24.9 us
  waiting for transfers between devices: 19.3 us -> 0 us
  matrix products: 18.8 us -> 0 us
  starting transfers between devices: 15 us -> 0 us
  between operations: 15.5 us -> 0.68 us
  local copies, waits for them, and re-layouts: 20.3 us -> 5.89 us
  Pallas kernels: 0 us -> 4.72 us
  other arithmetic: 3.27 us -> 0 us
    all_to_all x0 -> x2, blocking collectives: none -> 24.9 us  [the longest x1 15 us: local(): lax.all_to_all(sent.reshape(cores * spans, 2 * rows, width), ('vis', 'seq...]
    dot_general x97 -> x0, matrix products: 18.8 us -> none  [the longest x32 6.14 us: contract_cols(): lax.dot_general(left, right, (((1,), (1,)), ((), ())), preferred_element_...]
    all_to_all x2 -> x0, starting transfers between devices: 15 us -> none  [the longest x1 8.21 us: local(): lax.all_to_all(jnp.where(requested[None, :, None, None], selected, jnp.ze...]
    unnamed x2 -> x0, waiting for transfers between devices: 13.1 us -> none
    unnamed x45 -> x13, local copies, waits for them, and re-layouts: 13.8 us -> 4.55 us
    all_to_all x2 -> x0, waiting for transfers between devices: 6.2 us -> none  [the longest x1 6.2 us: local(): lax.all_to_all(partial_terms.astype(jnp.bfloat16), 'seq', split_axis=1, c...]
    pallas_call x0 -> x3, Pallas kernels: none -> 4.72 us  [the longest x1 3.85 us: local(): pl.pallas_call(functools.partial(attend_kernel, rows, per_owner, cores, s...]
    another operation x4 -> x0, local copies, waits for them, and re-layouts: 2.01 us -> none  [the longest x1 1.24 us: attend(): return (grad_query, jnp.stack(log_parts, axis=0), key_total, value_total)]
  transfers between devices with their start and end apart: 3 -> 0, of which waited for: 2 -> 0; matrix products, arithmetic and copies ran while one was open for 15% -> 0% of each run, Pallas kernels for 0% -> 0%
where the time goes in v1:
time: 36.6 us; the launch traced here: 36.2 us
  blocking collectives  24.9 us (68%)
  local copies, waits for them, and re-layouts  5.89 us (16%)
  Pallas kernels  4.72 us (13%)
  between operations  0.68 us (2%)
    all_to_all x1, blocking collectives, local(): lax.all_to_all(sent.reshape(cores * spans, 2 * rows, width), ('vis', 'seq...  15 us
    all_to_all x1, blocking collectives, local(): lax.all_to_all(terms.reshape(cores * spans, 2 * rows, width), ('vis', 'se...  9.9 us
    unnamed x13, local copies, waits for them, and re-layouts  4.55 us
    pallas_call x1, Pallas kernels, local(): pl.pallas_call(functools.partial(attend_kernel, rows, per_owner, cores, s...  3.85 us

profile of v1, /device:TPU:0, one launch (start us, length us, event | category | flops | bytes accessed | tf_op | source)
XLA Modules:
  0.0 36.2 jit_solution(2226249563563835083)
XLA Ops:
  0.6 0.0 copy-start.4
  0.6 0.0 copy-start.2
  0.7 0.7 %copy-done.4 = s32[16,8]{0,1:T(8,128)S(1)} copy-done((s32[16,8]{0,1:T(8,128)S(1)}, s32[16,8]{0,1:T(8,128)}, u32[]{:S(2)}) %copy-start.4) | copy-done | bytes 536
  1.3 0.1 copy.12.map_ref
  1.4 0.0 copy-start.5
  1.4 0.7 %copy-done.5 = s32[16]{0:T(128)S(1)} copy-done((s32[16]{0:T(128)S(1)}, s32[16]{0:T(128)}, u32[]{:S(2)}) %copy-start.5) | copy-done | bytes 88
  2.0 0.1 copy.13.count_ref
  2.1 0.0 copy-done.2
  2.1 0.0 copy-start.3
  2.1 0.7 %copy-done.3 = bf16[4,4,512]{2,1,0:T(4,128)(2,1)S(1)} copy-done((bf16[4,4,512]{2,1,0:T(4,128)(2,1)S(1)}, bf16[4,4,512]{2,1,0:T(4,128)(2,1)}, u32[]{:S(2)}) %copy-start.3) | copy-done | bytes 16408
  2.9 0.4 %choose_blocks.1 = bf16[2,128,256]{2,1,0:T(8,128)(2,1)S(1)} custom-call(s32[1]{0:T(128)} %bitcast.me_ref, s32[16,8]{1,0:T(8,128)S(1)} %copy.12.map_ref, s32[16,1]{1,0:T(8,128)S(1)} %copy.13.count_ref, bf16[16,512]{1,0:T(8,128)(2,1)S(1)} %reshape.40.keys_ref, bf16[16,512]{1,0:T(8,128)(2,1)S(1)} %reshape.41.values_ref), custom_call_target="tpu_custom_call" | custom-call | tf_op jit(solution)/shard_map/choose_blocks/pallas_call | solution.py:143
  3.3 15.0 %all_to_all.10 = bf16[32,8,256]{2,1,0:T(8,128)(2,1)S(1)} all-to-all(bf16[32,8,256]{2,1,0:T(8,128)(2,1)S(1)} %bitcast.8), channel_id=1, replica_groups=mesh['seq'=16,'vis'=2] {'vis','seq'}, dimensions={0} | all-to-all | bytes 262144 | tf_op jit(solution)/shard_map/all_to_all | solution.py:151
  18.3 0.0 copy-start
  18.3 1.2 %copy-done = bf16[256,2048]{1,0:T(8,128)(2,1)S(1)} copy-done((bf16[256,2048]{1,0:T(8,128)(2,1)S(1)}, bf16[256,2048]{1,0:T(8,128)(2,1)}, u32[]{:S(2)}) %copy-start) | copy-done | bytes 1048600
  19.5 0.0 copy-start.1
  19.5 1.2 %copy-done.1 = bf16[256,2048]{1,0:T(8,128)(2,1)S(1)} copy-done((bf16[256,2048]{1,0:T(8,128)(2,1)S(1)}, bf16[256,2048]{1,0:T(8,128)(2,1)}, u32[]{:S(2)}) %copy-start.1) | copy-done | bytes 1048600
  20.8 3.8 %attend.1 = (bf16[256,2048]{1,0:T(8,128)(2,1)}, f32[16,256]{1,0:T(8,128)}, bf16[256,256]{1,0:T(8,128)(2,1)S(1)}) custom-call(s32[1]{0:T(128)} %bitcast.me_ref, s32[16,8]{1,0:T(8,128)S(1)} %copy.12.map_ref, s32[16,1]{1,0:T(8,128)S(1)} %copy.13.count_ref, bf16[256,2048]{1,0:T(8,128)(2,1)S(1)} %copy-done, bf16[256,2048]{1,0:T(8,128)(2,1)S(1)} %copy-done.1, ...), custom_call_target="tpu_custom_call" | custom-call | tf_op jit(solution)/shard_map/attend/pallas_call | solution.py:154
  24.6 9.9 %all_to_all.11 = bf16[32,8,256]{2,1,0:T(8,128)(2,1)S(1)} all-to-all(bf16[32,8,256]{2,1,0:T(8,128)(2,1)S(1)} %bitcast.9), channel_id=1, replica_groups=mesh['seq'=16,'vis'=2] {'vis','seq'}, dimensions={0} | all-to-all | bytes 262144 | tf_op jit(solution)/shard_map/all_to_all | solution.py:166
  34.5 0.5 %sum_blocks.1 = (bf16[16,512]{1,0:T(8,128)(2,1)S(1)}, bf16[16,512]{1,0:T(8,128)(2,1)S(1)}) custom-call(s32[1]{0:T(128)} %bitcast.me_ref, s32[16,8]{1,0:T(8,128)S(1)} %copy.12.map_ref, s32[16,1]{1,0:T(8,128)S(1)} %copy.13.count_ref, bf16[2,128,256]{2,1,0:T(8,128)(2,1)S(1)} %bitcast.7), custom_call_target="tpu_custom_call" | custom-call | tf_op jit(solution)/shard_map/sum_blocks/pallas_call | solution.py:169
  35.0 0.6 %reshape.46 = bf16[4,4,512]{2,1,0:T(4,128)(2,1)} reshape(bf16[16,512]{1,0:T(8,128)(2,1)S(1)} %get-tuple-element.12) | data formatting | bytes 32768 | tf_op jit(solution)/shard_map/reshape | solution.py:177
  35.6 0.6 %reshape.47 = bf16[4,4,512]{2,1,0:T(4,128)(2,1)} reshape(bf16[16,512]{1,0:T(8,128)(2,1)S(1)} %get-tuple-element.13) | data formatting | bytes 32768 | tf_op jit(solution)/shard_map/reshape | solution.py:177
  (2 shorter events, 0.0 us)
Async XLA Ops:
  0.6 0.7 %copy-start.4 = (s32[16,8]{0,1:T(8,128)S(1)}, s32[16,8]{0,1:T(8,128)}, u32[]{:S(2)}) copy-start(s32[16,8]{0,1:T(8,128)} %param.10) | copy-start | bytes 1540
  0.6 1.5 %copy-start.2 = (bf16[4,4,512]{2,1,0:T(4,128)(2,1)S(1)}, bf16[4,4,512]{2,1,0:T(4,128)(2,1)}, u32[]{:S(2)}) copy-start(bf16[4,4,512]{2,1,0:T(4,128)(2,1)} %param.7) | copy-start | bytes 49156
  1.4 0.7 %copy-start.5 = (s32[16]{0:T(128)S(1)}, s32[16]{0:T(128)}, u32[]{:S(2)}) copy-start(s32[16]{0:T(128)} %param.11) | copy-start | bytes 196
  2.1 0.7 %copy-start.3 = (bf16[4,4,512]{2,1,0:T(4,128)(2,1)S(1)}, bf16[4,4,512]{2,1,0:T(4,128)(2,1)}, u32[]{:S(2)}) copy-start(bf16[4,4,512]{2,1,0:T(4,128)(2,1)} %param.8) | copy-start | bytes 49156
  18.3 1.2 %copy-start = (bf16[256,2048]{1,0:T(8,128)(2,1)S(1)}, bf16[256,2048]{1,0:T(8,128)(2,1)}, u32[]{:S(2)}) copy-start(bf16[256,2048]{1,0:T(8,128)(2,1)} %q_ref.1) | copy-start | bytes 3145732
  19.5 1.2 %copy-start.1 = (bf16[256,2048]{1,0:T(8,128)(2,1)S(1)}, bf16[256,2048]{1,0:T(8,128)(2,1)}, u32[]{:S(2)}) copy-start(bf16[256,2048]{1,0:T(8,128)(2,1)} %g_ref.1) | copy-start | bytes 3145732

commit v2 on v1

v2 whole, which is shorter than its diff:
```python
import functools
import math

import jax
import jax.numpy as jnp
from jax import lax
from jax.experimental import pallas as pl
from jax.experimental.pallas import tpu as pltpu
from jax.sharding import PartitionSpec as P

HEAD_DIM = 128
GROUP = 8
BF16 = jnp.bfloat16
F32 = jnp.float32
VMEM = pl.BlockSpec(memory_space=pltpu.VMEM)
HBM = pl.BlockSpec(memory_space=pltpu.HBM)
SMEM = pl.BlockSpec(memory_space=pltpu.SMEM)


def iota(shape, dim):
    return lax.broadcasted_iota(jnp.int32, shape, dim)


def dot(left, right, left_dim=1, right_dim=0):
    return lax.dot_general(
        left, right, (((left_dim,), (right_dim,)), ((), ())), preferred_element_type=F32
    )


def copy_all(pairs, sems):
    copies = [pltpu.make_async_copy(src, dst, sems.at[i]) for i, (src, dst) in enumerate(pairs)]
    for copy in copies:
        copy.start()
    for copy in copies:
        copy.wait()


def choose_kernel(
    width, starts, me_ref, map_hbm, count_hbm, keys_hbm, values_hbm, out_ref, pick_ref, map_ref, count_ref, keys_ref, values_ref, sems
):
    copy_all(
        ((map_hbm, map_ref), (count_hbm, count_ref), (keys_hbm, keys_ref), (values_hbm, values_ref)), sems
    )
    per_owner, rows, _ = keys_ref.shape
    most, spans = map_ref.shape
    block_map = map_ref[...]
    live = iota((most, spans), 0) < count_ref[...]
    asked = live & (block_map // per_owner == me_ref[0])
    slot = jnp.sum(jnp.where(asked, block_map % per_owner + 1, 0), axis=0, keepdims=True) - 1
    slot_rows, span_rows = pick_ref.shape
    expand = (iota((span_rows, spans), 0) // (2 * rows) == iota((span_rows, spans), 1)).astype(BF16)
    want = dot(jnp.broadcast_to(slot, (slot_rows, spans)).astype(F32).astype(BF16), expand, 1, 1)
    have, place = iota(pick_ref.shape, 0), iota(pick_ref.shape, 1) % (2 * rows)
    have_slot = have % (per_owner * rows) // rows
    have_place = have // (per_owner * rows) * rows + have % rows
    pick = ((want == have_slot.astype(F32)) & (place == have_place)).astype(BF16)
    pick_ref[...] = pick
    stacked = [ref[slot].astype(F32) for ref in (keys_ref, values_ref) for slot in range(per_owner)]
    stacked = jnp.concatenate(stacked, axis=0).astype(BF16)
    for core, start in enumerate(starts):
        out_ref[core] = dot(pick, stacked[:, start : start + width], 0, 0).astype(BF16)


def load_kernel(
    rows, per_owner, cores, me_ref, map_hbm, count_hbm, q_hbm, g_hbm, q_ref, g_ref, pick_ref, live_ref, map_ref, count_ref, sems
):
    copies = [pltpu.make_async_copy(src, dst, sems.at[2 + i]) for i, (src, dst) in enumerate(((q_hbm, q_ref), (g_hbm, g_ref)))]
    for copy in copies:
        copy.start()
    copy_all(((map_hbm, map_ref), (count_hbm, count_ref)), sems)
    most, spans = map_ref.shape
    block_rows = cores * rows
    keys = most * block_rows
    here = iota((1, spans), 1) == me_ref[0]
    owners = jnp.sum(jnp.where(here, map_ref[...] // per_owner, 0), axis=1, keepdims=True)
    count = jnp.sum(jnp.where(here, count_ref[...], 0), axis=1, keepdims=True)
    mine, theirs = iota((2 * keys, 1), 0), iota(pick_ref.shape, 1)
    block = mine % keys // block_rows
    expand = (iota((2 * keys, most), 1) == block).astype(BF16)
    lanes = 128
    owner = dot(expand, jnp.broadcast_to(owners, (most, lanes)).astype(F32).astype(BF16))[:, :1].astype(jnp.int32)
    place = ((mine % block_rows // rows * spans + owner) * 2 + mine // keys) * rows + mine % rows
    place = jnp.where(block < count, place, -1)
    pick_ref[...] = (place == theirs).astype(BF16)
    live_ref[...] = jnp.where(iota(live_ref.shape, 0) // block_rows < count, 0.0, -1e30)
    for copy in copies:
        copy.wait()


def block_diagonal(part):
    zero = jnp.zeros_like(part)
    return jnp.concatenate([jnp.concatenate([part, zero], 1), jnp.concatenate([zero, part], 1)], 0)


def attend_kernel(q_ref, g_ref, pick_ref, live_ref, rows_ref, terms_ref, gs_ref, k_ref, log_ref):
    score_scale = 1.0 / math.sqrt(HEAD_DIM)
    keys = k_ref.shape[0]
    kv_heads = k_ref.shape[1] // HEAD_DIM
    tokens = q_ref.shape[0]
    per_kv = q_ref.shape[1] // HEAD_DIM // kv_heads
    pick = pick_ref[...]
    fetched = dot(pick, rows_ref[...]).astype(BF16)
    k_ref[...] = fetched[:keys]
    live = live_ref[...]

    gk_parts, gv_parts = [], []
    for kv in range(kv_heads):
        cols = slice(kv * HEAD_DIM, (kv + 1) * HEAD_DIM)
        k2, v2 = block_diagonal(fetched[:keys, cols]), block_diagonal(fetched[keys:, cols])
        gk = jnp.zeros((2 * keys, 2 * HEAD_DIM), F32)
        gv = jnp.zeros((2 * keys, 2 * HEAD_DIM), F32)
        for pair in range(per_kv // 2):
            head = kv * per_kv + 2 * pair
            at = slice(head * HEAD_DIM, (head + 2) * HEAD_DIM)
            q, g = q_ref[:, at], g_ref[:, at]
            scores = (dot(k2, q, 1, 1) * score_scale).reshape(2, keys, tokens) + live
            row_max = jnp.max(scores, axis=1, keepdims=True)
            weights = jnp.exp(scores - row_max)
            totals = jnp.sum(weights, axis=1, keepdims=True)
            probs = weights * (1.0 / totals)
            log_ref[head : head + 2, :] = (row_max + jnp.log(totals)).reshape(2, tokens)
            low = probs.astype(BF16)
            grad_probs = dot(v2, g, 1, 1).reshape(2, keys, tokens)
            delta = jnp.sum(low.astype(F32) * grad_probs, axis=1, keepdims=True)
            gs = (probs * (grad_probs - delta)).astype(BF16).reshape(2 * keys, tokens)
            gs_ref[head // 2] = gs
            gv += dot(low.reshape(2 * keys, tokens), g)
            gk += dot(gs, q)
        gk_parts.append((gk[:keys, :HEAD_DIM] + gk[keys:, HEAD_DIM:]) * score_scale)
        gv_parts.append(gv[:keys, :HEAD_DIM] + gv[keys:, HEAD_DIM:])
    terms = jnp.concatenate([jnp.concatenate(gk_parts, 1), jnp.concatenate(gv_parts, 1)], 0).astype(BF16)
    terms_ref[...] = dot(pick, terms, 0, 0).astype(BF16)


def queries_kernel(gs_ref, k_ref, log_ref, out_hbm, log_hbm, out_ref, sems):
    score_scale = 1.0 / math.sqrt(HEAD_DIM)
    pairs = gs_ref.shape[0]
    kv_heads = k_ref.shape[1] // HEAD_DIM
    copies = [pltpu.make_async_copy(log_ref, log_hbm, sems.at[pairs])]
    copies[0].start()
    for kv in range(kv_heads):
        k2 = block_diagonal(k_ref[:, kv * HEAD_DIM : (kv + 1) * HEAD_DIM])
        for pair in range(kv * pairs // kv_heads, (kv + 1) * pairs // kv_heads):
            at = slice(2 * pair * HEAD_DIM, 2 * (pair + 1) * HEAD_DIM)
            out_ref[:, at] = (dot(gs_ref[pair], k2, 0, 0) * score_scale).astype(BF16)
            copies.append(pltpu.make_async_copy(out_ref.at[:, at], out_hbm.at[:, at], sems.at[pair]))
            copies[-1].start()
    for copy in copies:
        copy.wait()


def sum_kernel(width, starts, pick_ref, terms_ref, keys_ref, values_ref):
    per_owner, rows, _ = keys_ref.shape
    done = {}
    for core, start in enumerate(starts):
        part = dot(pick_ref[...], terms_ref[core])
        done[start] = done[start] + part if start in done else part
    for start, total in done.items():
        for slot in range(per_owner):
            for place, ref in ((slot, keys_ref), (per_owner + slot, values_ref)):
                ref[slot, :, start : start + width] = total[place * rows : (place + 1) * rows].astype(BF16)


def local(queries, keys, values, grad_out, block_map, block_count):
    spans, cores = lax.axis_size("seq"), lax.axis_size("vis")
    me = lax.axis_index("seq").astype(jnp.int32).reshape(1)
    per_owner, rows, _ = keys.shape
    tokens = queries.shape[0]
    heads = queries.shape[1] // HEAD_DIM
    most = block_map.shape[1]
    width = max(heads // GROUP, 1) * HEAD_DIM
    starts = tuple(core * heads // GROUP * HEAD_DIM for core in range(cores))
    attended = most * cores * rows
    block_map = block_map.T
    block_count = block_count.reshape(1, spans)
    stay = functools.partial(pltpu.with_memory_space_constraint, memory_space=pltpu.HBM)
    shape = jax.ShapeDtypeStruct
    params = pltpu.CompilerParams(vmem_limit_bytes=24 * 1024 * 1024)
    table_scratch = [pltpu.VMEM((most, spans), jnp.int32), pltpu.VMEM((1, spans), jnp.int32)]

    sent, pick = pl.pallas_call(
        functools.partial(choose_kernel, width, starts),
        out_shape=(
            shape((cores, spans * 2 * rows, width), BF16),
            shape((2 * per_owner * rows, spans * 2 * rows), BF16),
        ),
        in_specs=[SMEM, HBM, HBM, HBM, HBM],
        out_specs=(VMEM, VMEM),
        scratch_shapes=table_scratch
        + [pltpu.VMEM(keys.shape, BF16), pltpu.VMEM(keys.shape, BF16), pltpu.SemaphoreType.DMA((4,))],
        compiler_params=params,
        name="choose_blocks",
    )(me, stay(block_map), stay(block_count), stay(keys), stay(values))
    got = lax.all_to_all(
        sent.reshape(cores * spans, 2 * rows, width), ("vis", "seq"), split_axis=0, concat_axis=0, tiled=True
    )
    q, g, order, live = pl.pallas_call(
        functools.partial(load_kernel, rows, per_owner, cores),
        out_shape=(
            shape(queries.shape, BF16),
            shape(queries.shape, BF16),
            shape((2 * attended, cores * spans * 2 * rows), BF16),
            shape((attended, tokens), F32),
        ),
        in_specs=[SMEM, HBM, HBM, HBM, HBM],
        out_specs=(VMEM,) * 4,
        scratch_shapes=table_scratch + [pltpu.SemaphoreType.DMA((4,))],
        compiler_params=params,
        cost_estimate=pl.CostEstimate(flops=10**6, bytes_accessed=2 * queries.size * 4, transcendentals=0),
        name="load_operands",
    )(me, stay(block_map), stay(block_count), stay(queries), stay(grad_out))
    terms, gs, k, logs = pl.pallas_call(
        attend_kernel,
        out_shape=(
            shape((cores * spans * 2 * rows, width), BF16),
            shape((heads // 2, 2 * attended, tokens), BF16),
            shape((attended, width), BF16),
            shape((heads, tokens), F32),
        ),
        in_specs=[VMEM] * 5,
        out_specs=(VMEM,) * 4,
        compiler_params=params,
        name="attend",
    )(q, g, order, live, got.reshape(-1, width))
    back = lax.all_to_all(
        terms.reshape(cores * spans, 2 * rows, width), ("vis", "seq"), split_axis=0, concat_axis=0, tiled=True
    )
    grad_queries, log_totals = pl.pallas_call(
        queries_kernel,
        out_shape=(shape(queries.shape, BF16), shape((heads, tokens), F32)),
        in_specs=[VMEM] * 3,
        out_specs=(HBM, HBM),
        scratch_shapes=[pltpu.VMEM(queries.shape, BF16), pltpu.SemaphoreType.DMA((heads // 2 + 1,))],
        compiler_params=params,
        cost_estimate=pl.CostEstimate(
            flops=4 * tokens * attended * heads * HEAD_DIM, bytes_accessed=4 * queries.size, transcendentals=0
        ),
        name="grad_queries",
    )(gs, k, logs)
    grad_keys, grad_values = pl.pallas_call(
        functools.partial(sum_kernel, width, starts),
        out_shape=(shape(keys.shape, BF16),) * 2,
        in_specs=[VMEM, VMEM],
        out_specs=(VMEM, VMEM),
        compiler_params=params,
        name="sum_blocks",
    )(pick, back.reshape(cores, -1, width))
    return grad_queries, log_totals, grad_keys, grad_values


def solution(mesh):
    in_specs = (
        P("seq", "vis"),
        P("seq", "vis", None),
        P("seq", "vis", None),
        P("seq", "vis"),
        P(),
        P(),
    )
    out_specs = (P("seq", "vis"), P("vis", "seq"), P("seq", "vis", None), P("seq", "vis", None))
    return jax.shard_map(local, mesh=mesh, in_specs=in_specs, out_specs=out_specs, check_vma=False)
```

time: 36.6 us -> 32.2 us (0.88)
  blocking collectives: 24.9 us -> 0 us
  waiting for transfers between devices: 0 us -> 12.8 us
  starting transfers between devices: 0 us -> 9.88 us
  local copies, waits for them, and re-layouts: 5.89 us -> 0 us
  Pallas kernels: 4.72 us -> 8.45 us
    all_to_all x2 -> x0, blocking collectives: 24.9 us -> none  [the longest x1 15 us: local(): lax.all_to_all(sent.reshape(cores * spans, 2 * rows, width), ('vis', 'seq...]
    all_to_all x0 -> x2, waiting for transfers between devices: none -> 12.8 us  [the longest x1 6.61 us: local(): lax.all_to_all(terms.reshape(cores * spans, 2 * rows, width), ('vis', 'se...]
    all_to_all x0 -> x2, starting transfers between devices: none -> 9.88 us  [the longest x1 7.3 us: local(): lax.all_to_all(sent.reshape(cores * spans, 2 * rows, width), ('vis', 'seq...]
    unnamed x13 -> x0, local copies, waits for them, and re-layouts: 4.55 us -> none
    pallas_call x3 -> x5, Pallas kernels: 4.72 us -> 8.45 us  [the longest x1 2.87 us: local(): pl.pallas_call(attend_kernel, out_shape=(shape((cores * spans * 2 * rows,...]
    reshape x5 -> x0, local copies, waits for them, and re-layouts: 1.35 us -> none  [the longest x1 0.62 us: local(): grad_keys.reshape(keys.shape)]
  transfers between devices with their start and end apart: 0 -> 2, of which waited for: 0 -> 2; matrix products, arithmetic and copies ran while one was open for 0% -> 0% of each run, Pallas kernels for 0% -> 9%
where the time goes in v2:
time: 32.2 us; the launch traced here: 31.8 us
  waiting for transfers between devices  12.8 us (40%)
  starting transfers between devices  9.88 us (31%)
  Pallas kernels  8.45 us (26%)
  between operations  0.68 us (2%)
    all_to_all x1, starting transfers between devices, local(): lax.all_to_all(sent.reshape(cores * spans, 2 * rows, width), ('vis', 'seq...  7.3 us
    all_to_all x1, waiting for transfers between devices, local(): lax.all_to_all(terms.reshape(cores * spans, 2 * rows, width), ('vis', 'se...  6.61 us
    all_to_all x1, waiting for transfers between devices, local(): lax.all_to_all(sent.reshape(cores * spans, 2 * rows, width), ('vis', 'seq...  6.2 us
    pallas_call x1, Pallas kernels, local(): pl.pallas_call(attend_kernel, out_shape=(shape((cores * spans * 2 * rows,...  2.87 us
    all_to_all x1, starting transfers between devices, local(): lax.all_to_all(terms.reshape(cores * spans, 2 * rows, width), ('vis', 'se...  2.57 us
    pallas_call x1, Pallas kernels, local(): pl.pallas_call(functools.partial(choose_kernel, width, starts), out_shape...  1.84 us
    pallas_call x1, Pallas kernels, local(): pl.pallas_call(functools.partial(load_kernel, rows, per_owner, cores), ou...  1.7 us
    pallas_call x1, Pallas kernels, local(): pl.pallas_call(queries_kernel, out_shape=(shape(queries.shape, BF16), sha...  1.3 us
  transfers between devices with their start and end apart: 2, of which 2 were waited for; matrix products, arithmetic and copies ran while one was open for 0% of the time, Pallas kernels for 9%

profile of v2, /device:TPU:0, one launch (start us, length us, event | category | flops | bytes accessed | tf_op | source)
XLA Modules:
  0.0 31.8 jit_solution(15365576200125325114)
XLA Ops:
  0.6 1.8 %choose_blocks.1 = (bf16[2,128,256]{2,1,0:T(8,128)(2,1)}, bf16[32,128]{1,0:T(8,128)(2,1)S(1)}) custom-call(s32[1]{0:T(128)} %bitcast.me_ref, s32[8,16]{1,0:T(8,128)} %bitcast.9, s32[1,16]{1,0:T(1,128)} %bitcast.11, bf16[4,4,512]{2,1,0:T(4,128)(2,1)} %keys_hbm.1, bf16[4,4,512]{2,1,0:T(4,128)(2,1)} %values_hbm.1), custom_call_target="tpu_custom_call" | custom-call | tf_op jit(solution)/shard_map/choose_blocks/pallas_call | solution.py:181
  2.5 7.3 %all-to-all-start = ((bf16[32,8,256]{2,1,0:T(8,128)(2,1)}), bf16[32,8,256]{2,1,0:T(8,128)(2,1)S(1)}, u32[]{:S(2)}, u32[]{:S(2)}) async-start(bf16[32,8,256]{2,1,0:T(8,128)(2,1)} %bitcast.3), calls=%async_computation | async-start | bytes 262144 | tf_op jit(solution)/shard_map/all_to_all | solution.py:194
  9.8 1.7 %load_operands.1 = (bf16[256,2048]{1,0:T(8,128)(2,1)S(1)}, bf16[256,2048]{1,0:T(8,128)(2,1)S(1)}, bf16[128,256]{1,0:T(8,128)(2,1)S(1)}, f32[64,256]{1,0:T(8,128)S(1)}) custom-call(s32[1]{0:T(128)} %bitcast.me_ref, s32[8,16]{1,0:T(8,128)} %bitcast.10, s32[1,16]{1,0:T(1,128)} %bitcast.12, bf16[256,2048]{1,0:T(8,128)(2,1)} %q_hbm.1, bf16[256,2048]{1,0:T(8,128)(2,1)} %g_hbm.1), custom_call_target="tpu_custom_call" | custom-call | flops 1000000 | bytes 4194304 | tf_op jit(solution)/shard_map/load_operands/pallas_call | solution.py:197
  11.5 6.2 %all-to-all-done = bf16[32,8,256]{2,1,0:T(8,128)(2,1)S(1)} async-done(((bf16[32,8,256]{2,1,0:T(8,128)(2,1)}), bf16[32,8,256]{2,1,0:T(8,128)(2,1)S(1)}, u32[]{:S(2)}, u32[]{:S(2)}) %all-to-all-start) | async-done | bytes 131104 | tf_op jit(solution)/shard_map/all_to_all | solution.py:194
  17.7 2.9 %attend.1 = (bf16[256,256]{1,0:T(8,128)(2,1)}, bf16[8,128,256]{2,1,0:T(8,128)(2,1)S(1)}, bf16[64,256]{1,0:T(8,128)(2,1)S(1)}, f32[16,256]{1,0:T(8,128)S(1)}) custom-call(bf16[256,2048]{1,0:T(8,128)(2,1)S(1)} %get-tuple-element.18.q_ref, bf16[256,2048]{1,0:T(8,128)(2,1)S(1)} %get-tuple-element.19.g_ref, bf16[128,256]{1,0:T(8,128)(2,1)S(1)} %get-tuple-element.20.pick_ref, ...), custom_call_target="tpu_custom_call" | custom-call | tf_op jit(solution)/shard_map/attend/pallas_call | solution.py:212
  20.6 2.6 %all-to-all-start.1 = ((bf16[32,8,256]{2,1,0:T(8,128)(2,1)}), bf16[32,8,256]{2,1,0:T(8,128)(2,1)S(1)}, u32[]{:S(2)}, u32[]{:S(2)}) async-start(bf16[32,8,256]{2,1,0:T(8,128)(2,1)} %bitcast.5), calls=%async_computation.1 | async-start | bytes 262144 | tf_op jit(solution)/shard_map/all_to_all | solution.py:225
  23.2 1.3 %grad_queries.1 = (bf16[256,2048]{1,0:T(8,128)(2,1)}, f32[16,256]{1,0:T(8,128)}) custom-call(bf16[8,128,256]{2,1,0:T(8,128)(2,1)S(1)} %get-tuple-element.23.gs_ref, bf16[64,256]{1,0:T(8,128)(2,1)S(1)} %get-tuple-element.24.k_ref, f32[16,256]{1,0:T(8,128)S(1)} %get-tuple-element.25.log_ref), custom_call_target="tpu_custom_call" | custom-call | flops 134217728 | bytes 2097152 | tf_op jit(solution)/shard_map/grad_queries/pallas_call | solution.py:228
  24.5 6.6 %all-to-all-done.1 = bf16[32,8,256]{2,1,0:T(8,128)(2,1)S(1)} async-done(((bf16[32,8,256]{2,1,0:T(8,128)(2,1)}), bf16[32,8,256]{2,1,0:T(8,128)(2,1)S(1)}, u32[]{:S(2)}, u32[]{:S(2)}) %all-to-all-start.1) | async-done | bytes 131104 | tf_op jit(solution)/shard_map/all_to_all | solution.py:225
  31.1 0.7 %sum_blocks.1 = (bf16[4,4,512]{2,1,0:T(4,128)(2,1)}, bf16[4,4,512]{2,1,0:T(4,128)(2,1)}) custom-call(bf16[32,128]{1,0:T(8,128)(2,1)S(1)} %get-tuple-element.28.pick_ref, bf16[2,128,256]{2,1,0:T(8,128)(2,1)S(1)} %bitcast.8), custom_call_target="tpu_custom_call" | custom-call | tf_op jit(solution)/shard_map/sum_blocks/pallas_call | solution.py:240
Async XLA Ops:
  2.5 15.2 %all-to-all-start = ((bf16[32,8,256]{2,1,0:T(8,128)(2,1)}), bf16[32,8,256]{2,1,0:T(8,128)(2,1)S(1)}, u32[]{:S(2)}, u32[]{:S(2)}) async-start(bf16[32,8,256]{2,1,0:T(8,128)(2,1)} %bitcast.3), calls=%async_computation | async-start | bytes 262144 | tf_op jit(solution)/shard_map/all_to_all | solution.py:194
  20.6 10.5 %all-to-all-start.1 = ((bf16[32,8,256]{2,1,0:T(8,128)(2,1)}), bf16[32,8,256]{2,1,0:T(8,128)(2,1)S(1)}, u32[]{:S(2)}, u32[]{:S(2)}) async-start(bf16[32,8,256]{2,1,0:T(8,128)(2,1)} %bitcast.5), calls=%async_computation.1 | async-start | bytes 262144 | tf_op jit(solution)/shard_map/all_to_all | solution.py:225

commit v3 on v2

v3 whole, which is shorter than its diff:
```python
import functools
import math

import jax
import jax.numpy as jnp
from jax import lax
from jax.experimental import pallas as pl
from jax.experimental.pallas import tpu as pltpu
from jax.sharding import PartitionSpec as P

HEAD_DIM = 128
GROUP = 8
BF16 = jnp.bfloat16
F32 = jnp.float32
LOG2E = math.log2(math.e)
VMEM = pl.BlockSpec(memory_space=pltpu.VMEM)
HBM = pl.BlockSpec(memory_space=pltpu.HBM)
SMEM = pl.BlockSpec(memory_space=pltpu.SMEM)


def iota(shape, dim):
    return lax.broadcasted_iota(jnp.int32, shape, dim)


def dot(left, right, left_dim=1, right_dim=0):
    return lax.dot_general(
        left, right, (((left_dim,), (right_dim,)), ((), ())), preferred_element_type=F32
    )


def choose_kernel(
    width, starts, me_ref, map_hbm, count_hbm, keys_hbm, values_hbm, q_hbm, g_hbm,
    out_ref, pick_ref, order_ref, live_ref, q_ref, g_ref, map_ref, count_ref, keys_ref, values_ref, sems
):
    pairs = (
        (map_hbm, map_ref), (count_hbm, count_ref), (keys_hbm, keys_ref), (values_hbm, values_ref), (q_hbm, q_ref), (g_hbm, g_ref)
    )
    copies = [pltpu.make_async_copy(src, dst, sems.at[i]) for i, (src, dst) in enumerate(pairs)]
    for copy in copies:
        copy.start()
    me = me_ref[0]
    per_owner, rows, _ = keys_ref.shape
    most, spans = map_ref.shape
    cores = len(starts)

    slot_rows, span_rows = pick_ref.shape
    expand_spans = (iota((span_rows, spans), 0) // (2 * rows) == iota((span_rows, spans), 1)).astype(BF16)
    have, place = iota((slot_rows, 1), 0), iota((1, span_rows), 1) % (2 * rows)
    have_slot = (have % (per_owner * rows) // rows + 1).astype(F32)
    have_place = have // (per_owner * rows) * rows + have % rows
    same_place = have_place == place

    block_rows = cores * rows
    keys = most * block_rows
    mine, theirs = iota((2 * keys, 1), 0), iota(order_ref.shape, 1)
    block = mine % keys // block_rows
    expand_blocks = (iota((2 * keys, most), 1) == block).astype(BF16)
    offset = mine % block_rows // rows * (spans * 2 * rows) + mine // keys * rows + mine % rows
    here = iota((1, spans), 1) == me
    live_block = iota(live_ref.shape, 0) // block_rows

    for copy in copies[:4]:
        copy.wait()
    relative = map_ref[...] - me * per_owner
    asked = (relative >= 0) & (relative < per_owner) & (iota((most, spans), 0) < count_ref[...])
    slot = jnp.sum(jnp.where(asked, relative + 1, 0), axis=0, keepdims=True).astype(F32)
    want = dot(jnp.broadcast_to(slot, (slot_rows, spans)).astype(BF16), expand_spans, 1, 1)
    pick = ((want == have_slot) & same_place).astype(BF16)
    stacked = [ref[slot].astype(F32) for ref in (keys_ref, values_ref) for slot in range(per_owner)]
    stacked = jnp.concatenate(stacked, axis=0).astype(BF16)
    for core, start in enumerate(starts):
        out_ref[core] = dot(pick, stacked[:, start : start + width], 0, 0).astype(BF16)
    pick_ref[...] = pick

    owners = jnp.sum(jnp.where(here, map_ref[...] // per_owner, 0), axis=1, keepdims=True)
    count = jnp.sum(jnp.where(here, count_ref[...], 0), axis=1, keepdims=True)
    lanes = jnp.broadcast_to(owners.astype(F32), (most, order_ref.shape[1])).astype(BF16)
    owner = dot(expand_blocks, lanes).astype(jnp.int32)
    travels = jnp.where(block < count, offset, -theirs.shape[1] * most * spans) + owner * (2 * rows)
    order_ref[...] = (travels == theirs).astype(BF16)
    live_ref[...] = jnp.where(live_block < count, 0.0, -1e30)
    for copy in copies[4:]:
        copy.wait()


def block_diagonal(part):
    zero = jnp.zeros_like(part)
    return jnp.concatenate([jnp.concatenate([part, zero], 1), jnp.concatenate([zero, part], 1)], 0)


def attend_kernel(
    q_ref, g_ref, order_ref, live_ref, rows_ref, terms_ref, gq_hbm, log_hbm,
    scores_ref, gp_ref, probs_ref, low_ref, gs_ref, gq_ref, log_ref, sems
):
    score_scale = 1.0 / math.sqrt(HEAD_DIM)
    keys, tokens = live_ref.shape
    kv_heads = rows_ref.shape[1] // HEAD_DIM
    pairs = gs_ref.shape[0]
    split, joined = (2, keys, tokens), (2 * keys, tokens)
    columns = [slice(2 * pair * HEAD_DIM, 2 * (pair + 1) * HEAD_DIM) for pair in range(pairs)]
    order, live = order_ref[...], live_ref[...]
    fetched = dot(order, rows_ref[...]).astype(BF16)
    heads = [fetched[:, kv * HEAD_DIM : (kv + 1) * HEAD_DIM] for kv in range(kv_heads)]
    k2 = [block_diagonal(head[:keys]) for head in heads for _ in range(pairs // kv_heads)]
    v2 = [block_diagonal(head[keys:]) for head in heads for _ in range(pairs // kv_heads)]

    for pair, at in enumerate(columns):
        scores_ref[pair] = dot(k2[pair], q_ref[:, at], 1, 1)
    for pair in range(pairs):
        scores = scores_ref[pair].reshape(split) * (score_scale * LOG2E) + live
        row_max = jnp.max(scores, axis=1, keepdims=True)
        weights = jnp.exp2(scores - row_max)
        totals = jnp.sum(weights, axis=1, keepdims=True)
        probs = weights * (1.0 / totals)
        log_ref[2 * pair : 2 * pair + 2, :] = ((row_max + jnp.log2(totals)) * (1.0 / LOG2E)).reshape(2, tokens)
        probs_ref[pair] = probs.reshape(joined)
        low_ref[pair] = probs.astype(BF16).reshape(joined)
    copies = [pltpu.make_async_copy(log_ref, log_hbm, sems.at[pairs])]
    copies[0].start()
    for pair, at in enumerate(columns):
        gp_ref[pair] = dot(v2[pair], g_ref[:, at], 1, 1)
    for pair in range(pairs):
        grad_probs = gp_ref[pair].reshape(split)
        delta = jnp.sum(low_ref[pair].reshape(split).astype(F32) * grad_probs, axis=1, keepdims=True)
        gs_ref[pair] = (probs_ref[pair].reshape(split) * (grad_probs - delta)).astype(BF16).reshape(joined)
    for pair, at in enumerate(columns):
        gq_ref[:, at] = (dot(gs_ref[pair], k2[pair], 0, 0) * score_scale).astype(BF16)
        copies.append(pltpu.make_async_copy(gq_ref.at[:, at], gq_hbm.at[:, at], sems.at[pair]))
        copies[-1].start()
    gk, gv = [0.0] * kv_heads, [0.0] * kv_heads
    for pair, at in enumerate(columns):
        kv = pair * kv_heads // pairs
        gk[kv] += dot(gs_ref[pair], q_ref[:, at])
        gv[kv] += dot(low_ref[pair], g_ref[:, at])
    gk = [(part[:keys, :HEAD_DIM] + part[keys:, HEAD_DIM:]) * score_scale for part in gk]
    gv = [part[:keys, :HEAD_DIM] + part[keys:, HEAD_DIM:] for part in gv]
    terms = jnp.concatenate([jnp.concatenate(gk, 1), jnp.concatenate(gv, 1)], 0).astype(BF16)
    terms_ref[...] = dot(order, terms, 0, 0).astype(BF16)
    for copy in copies:
        copy.wait()


def sum_kernel(width, starts, pick_ref, terms_ref, keys_ref, values_ref):
    per_owner, rows, _ = keys_ref.shape
    done = {}
    for core, start in enumerate(starts):
        part = dot(pick_ref[...], terms_ref[core])
        done[start] = done[start] + part if start in done else part
    for start, total in done.items():
        for slot in range(per_owner):
            for place, ref in ((slot, keys_ref), (per_owner + slot, values_ref)):
                ref[slot, :, start : start + width] = total[place * rows : (place + 1) * rows].astype(BF16)


def local(queries, keys, values, grad_out, block_map, block_count):
    spans, cores = lax.axis_size("seq"), lax.axis_size("vis")
    me = lax.axis_index("seq").astype(jnp.int32).reshape(1)
    per_owner, rows, _ = keys.shape
    tokens = queries.shape[0]
    heads = queries.shape[1] // HEAD_DIM
    most = block_map.shape[1]
    width = max(heads // GROUP, 1) * HEAD_DIM
    starts = tuple(core * heads // GROUP * HEAD_DIM for core in range(cores))
    attended = most * cores * rows
    travelling = spans * 2 * rows
    shape = jax.ShapeDtypeStruct
    params = pltpu.CompilerParams(vmem_limit_bytes=24 * 1024 * 1024)
    stay = functools.partial(pltpu.with_memory_space_constraint, memory_space=pltpu.HBM)

    sent, pick, order, live, q, g = pl.pallas_call(
        functools.partial(choose_kernel, width, starts),
        out_shape=(
            shape((cores, travelling, width), BF16),
            shape((2 * per_owner * rows, travelling), BF16),
            shape((2 * attended, cores * travelling), BF16),
            shape((attended, tokens), F32),
            shape(queries.shape, BF16),
            shape(queries.shape, BF16),
        ),
        in_specs=[SMEM] + [HBM] * 6,
        out_specs=(VMEM,) * 6,
        scratch_shapes=[
            pltpu.VMEM((most, spans), jnp.int32),
            pltpu.VMEM((1, spans), jnp.int32),
            pltpu.VMEM(keys.shape, BF16),
            pltpu.VMEM(keys.shape, BF16),
            pltpu.SemaphoreType.DMA((6,)),
        ],
        compiler_params=params,
        name="choose_blocks",
    )(me, *map(stay, (block_map.T, block_count.reshape(1, spans), keys, values, queries, grad_out)))
    got = lax.all_to_all(
        sent.reshape(cores * spans, 2 * rows, width), ("vis", "seq"), split_axis=0, concat_axis=0, tiled=True
    )
    pair_shape = (heads // 2, 2 * attended, tokens)
    terms, grad_queries, log_totals = pl.pallas_call(
        attend_kernel,
        out_shape=(
            shape((cores * travelling, width), BF16),
            shape(queries.shape, BF16),
            shape((heads, tokens), F32),
        ),
        in_specs=[VMEM] * 5,
        out_specs=(VMEM, HBM, HBM),
        scratch_shapes=[pltpu.VMEM(pair_shape, kind) for kind in (F32, F32, F32, BF16, BF16)]
        + [
            pltpu.VMEM(queries.shape, BF16),
            pltpu.VMEM((heads, tokens), F32),
            pltpu.SemaphoreType.DMA((heads // 2 + 1,)),
        ],
        compiler_params=params,
        name="attend",
    )(q, g, order, live, got.reshape(-1, width))
    back = lax.all_to_all(
        terms.reshape(cores * spans, 2 * rows, width), ("vis", "seq"), split_axis=0, concat_axis=0, tiled=True
    )
    grad_keys, grad_values = pl.pallas_call(
        functools.partial(sum_kernel, width, starts),
        out_shape=(shape(keys.shape, BF16),) * 2,
        in_specs=[VMEM, VMEM],
        out_specs=(VMEM, VMEM),
        compiler_params=params,
        name="sum_blocks",
    )(pick, back.reshape(cores, -1, width))
    return grad_queries, log_totals, grad_keys, grad_values


def solution(mesh):
    in_specs = (
        P("seq", "vis"),
        P("seq", "vis", None),
        P("seq", "vis", None),
        P("seq", "vis"),
        P(),
        P(),
    )
    out_specs = (P("seq", "vis"), P("vis", "seq"), P("seq", "vis", None), P("seq", "vis", None))
    return jax.shard_map(local, mesh=mesh, in_specs=in_specs, out_specs=out_specs, check_vma=False)
```

time: 32.2 us -> 30.3 us (0.941)
  blocking collectives: 0 us -> 24.9 us
  waiting for transfers between devices: 12.8 us -> 0 us
  starting transfers between devices: 9.88 us -> 0 us
  Pallas kernels: 8.45 us -> 4.54 us
    all_to_all x0 -> x2, blocking collectives: none -> 24.9 us  [the longest x1 15 us: local(): lax.all_to_all(sent.reshape(cores * spans, 2 * rows, width), ('vis', 'seq...]
    all_to_all x2 -> x0, waiting for transfers between devices: 12.8 us -> none  [the longest x1 6.61 us: local(): lax.all_to_all(terms.reshape(cores * spans, 2 * rows, width), ('vis', 'se...]
    all_to_all x2 -> x0, starting transfers between devices: 9.88 us -> none  [the longest x1 7.3 us: local(): lax.all_to_all(sent.reshape(cores * spans, 2 * rows, width), ('vis', 'seq...]
    pallas_call x3 -> x1, Pallas kernels: 5.86 us -> 2.13 us  [local(): pl.pallas_call(attend_kernel, out_shape=(shape((cores * travelling, width...]
  transfers between devices with their start and end apart: 2 -> 0, of which waited for: 2 -> 0; matrix products, arithmetic and copies ran while one was open for 0% -> 0% of each run, Pallas kernels for 9% -> 0%
where the time goes in v3:
time: 30.3 us; the launch traced here: 30.1 us
  blocking collectives  24.9 us (82%)
  Pallas kernels  4.54 us (15%)
  between operations  0.65 us (2%)
    all_to_all x1, blocking collectives, local(): lax.all_to_all(sent.reshape(cores * spans, 2 * rows, width), ('vis', 'seq...  15 us
    all_to_all x1, blocking collectives, local(): lax.all_to_all(terms.reshape(cores * spans, 2 * rows, width), ('vis', 'se...  9.91 us
    pallas_call x1, Pallas kernels, local(): pl.pallas_call(attend_kernel, out_shape=(shape((cores * travelling, width...  2.13 us
    pallas_call x1, Pallas kernels, local(): pl.pallas_call(functools.partial(choose_kernel, width, starts), out_shape...  1.66 us
    pallas_call x1, Pallas kernels, local(): pl.pallas_call(functools.partial(sum_kernel, width, starts), out_shape=(s...  0.75 us

profile of v3, /device:TPU:0, one launch (start us, length us, event | category | flops | bytes accessed | tf_op | source)
XLA Modules:
  0.0 30.1 jit_solution(4763564470832308027)
XLA Ops:
  0.6 1.7 %choose_blocks.1 = (bf16[2,128,256]{2,1,0:T(8,128)(2,1)S(1)}, bf16[32,128]{1,0:T(8,128)(2,1)S(1)}, bf16[128,256]{1,0:T(8,128)(2,1)S(1)}, f32[64,256]{1,0:T(8,128...) custom-call(s32[1]{0:T(128)} %bitcast.me_ref, s32[8,16]{1,0:T(8,128)} %bitcast.11, s32[1,16]{1,0:T(1,128)} %bitcast.12, ...), custom_call_target="tpu_custom_call" | custom-call | tf_op jit(solution)/shard_map/choose_blocks/pallas_call | solution.py:170
  2.3 15.0 %all_to_all.10 = bf16[32,8,256]{2,1,0:T(8,128)(2,1)S(1)} all-to-all(bf16[32,8,256]{2,1,0:T(8,128)(2,1)S(1)} %bitcast.10), channel_id=1, replica_groups=mesh['seq'=16,'vis'=2] {'vis','seq'}, dimensions={0} | all-to-all | bytes 262144 | tf_op jit(solution)/shard_map/all_to_all | solution.py:192
  17.3 2.1 %attend.1 = (bf16[256,256]{1,0:T(8,128)(2,1)S(1)}, bf16[256,2048]{1,0:T(8,128)(2,1)}, f32[16,256]{1,0:T(8,128)}) custom-call(bf16[256,2048]{1,0:T(8,128)(2,1)S(1)} %get-tuple-element.15.q_ref, bf16[256,2048]{1,0:T(8,128)(2,1)S(1)} %get-tuple-element.16.g_ref, bf16[128,256]{1,0:T(8,128)(2,1)S(1)} %get-tuple-element.17.order_ref, ...), custom_call_target="tpu_custom_call" | custom-call | tf_op jit(solution)/shard_map/attend/pallas_call | solution.py:196
  19.5 9.9 %all_to_all.11 = bf16[32,8,256]{2,1,0:T(8,128)(2,1)S(1)} all-to-all(bf16[32,8,256]{2,1,0:T(8,128)(2,1)S(1)} %bitcast.9), channel_id=1, replica_groups=mesh['seq'=16,'vis'=2] {'vis','seq'}, dimensions={0} | all-to-all | bytes 262144 | tf_op jit(solution)/shard_map/all_to_all | solution.py:214
  29.4 0.7 %sum_blocks.1 = (bf16[4,4,512]{2,1,0:T(4,128)(2,1)}, bf16[4,4,512]{2,1,0:T(4,128)(2,1)}) custom-call(bf16[32,128]{1,0:T(8,128)(2,1)S(1)} %get-tuple-element.22.pick_ref, bf16[2,128,256]{2,1,0:T(8,128)(2,1)S(1)} %bitcast.8), custom_call_target="tpu_custom_call" | custom-call | tf_op jit(solution)/shard_map/sum_blocks/pallas_call | solution.py:217

commit v4 on v3

--- a/solution.py
+++ b/solution.py
@@ -88,9 +88,18 @@
     return jnp.concatenate([jnp.concatenate([part, zero], 1), jnp.concatenate([zero, part], 1)], 0)
 
 
-def attend_kernel(
-    q_ref, g_ref, order_ref, live_ref, rows_ref, terms_ref, gq_hbm, log_hbm,
-    scores_ref, gp_ref, probs_ref, low_ref, gs_ref, gq_ref, log_ref, sems
+def grad_queries_of(pair, gs_ref, k2, gq_ref, gq_hbm, sem):
+    score_scale = 1.0 / math.sqrt(HEAD_DIM)
+    at = slice(2 * pair * HEAD_DIM, 2 * (pair + 1) * HEAD_DIM)
+    gq_ref[:, at] = (dot(gs_ref[pair], k2, 0, 0) * score_scale).astype(BF16)
+    copy = pltpu.make_async_copy(gq_ref.at[:, at], gq_hbm.at[:, at], sem)
+    copy.start()
+    return copy
+
+
+def attend_body(
+    early, q_ref, g_ref, order_ref, live_ref, rows_ref, terms_ref, gq_hbm, log_ref, gs_ref, k_ref,
+    scores_ref, gp_ref, probs_ref, low_ref, gq_ref, sems
 ):
     score_scale = 1.0 / math.sqrt(HEAD_DIM)
     keys, tokens = live_ref.shape
@@ -100,6 +109,7 @@
     columns = [slice(2 * pair * HEAD_DIM, 2 * (pair + 1) * HEAD_DIM) for pair in range(pairs)]
     order, live = order_ref[...], live_ref[...]
     fetched = dot(order, rows_ref[...]).astype(BF16)
+    k_ref[...] = fetched[:keys]
     heads = [fetched[:, kv * HEAD_DIM : (kv + 1) * HEAD_DIM] for kv in range(kv_heads)]
     k2 = [block_diagonal(head[:keys]) for head in heads for _ in range(pairs // kv_heads)]
     v2 = [block_diagonal(head[keys:]) for head in heads for _ in range(pairs // kv_heads)]
@@ -115,18 +125,16 @@
         log_ref[2 * pair : 2 * pair + 2, :] = ((row_max + jnp.log2(totals)) * (1.0 / LOG2E)).reshape(2, tokens)
         probs_ref[pair] = probs.reshape(joined)
         low_ref[pair] = probs.astype(BF16).reshape(joined)
-    copies = [pltpu.make_async_copy(log_ref, log_hbm, sems.at[pairs])]
-    copies[0].start()
+    copies = []
     for pair, at in enumerate(columns):
         gp_ref[pair] = dot(v2[pair], g_ref[:, at], 1, 1)
     for pair in range(pairs):
         grad_probs = gp_ref[pair].reshape(split)
         delta = jnp.sum(low_ref[pair].reshape(split).astype(F32) * grad_probs, axis=1, keepdims=True)
         gs_ref[pair] = (probs_ref[pair].reshape(split) * (grad_probs - delta)).astype(BF16).reshape(joined)
-    for pair, at in enumerate(columns):
-        gq_ref[:, at] = (dot(gs_ref[pair], k2[pair], 0, 0) * score_scale).astype(BF16)
-        copies.append(pltpu.make_async_copy(gq_ref.at[:, at], gq_hbm.at[:, at], sems.at[pair]))
-        copies[-1].start()
+    if early:
+        for pair in range(pairs):
+            copies.append(grad_queries_of(pair, gs_ref, k2[pair], gq_ref, gq_hbm, sems.at[pair]))
     gk, gv = [0.0] * kv_heads, [0.0] * kv_heads
     for pair, at in enumerate(columns):
         kv = pair * kv_heads // pairs
@@ -140,7 +148,15 @@
         copy.wait()
 
 
-def sum_kernel(width, starts, pick_ref, terms_ref, keys_ref, values_ref):
+def attend_kernel(me_ref, *refs):
+    pl.when(me_ref[0] == 0)(lambda: attend_body(True, *refs))
+    pl.when(me_ref[0] != 0)(lambda: attend_body(False, *refs))
+
+
+def sum_kernel(
+    width, starts, me_ref, pick_ref, terms_ref, gs_ref, k_ref, log_ref, _, keys_hbm, values_hbm, log_hbm, gq_hbm,
+    keys_ref, values_ref, gq_ref, sems
+):
     per_owner, rows, _ = keys_ref.shape
     done = {}
     for core, start in enumerate(starts):
@@ -150,6 +166,28 @@
         for slot in range(per_owner):
             for place, ref in ((slot, keys_ref), (per_owner + slot, values_ref)):
                 ref[slot, :, start : start + width] = total[place * rows : (place + 1) * rows].astype(BF16)
+    pairs = gs_ref.shape[0]
+    copies = [
+        pltpu.make_async_copy(keys_ref, keys_hbm, sems.at[pairs]),
+        pltpu.make_async_copy(values_ref, values_hbm, sems.at[pairs + 1]),
+        pltpu.make_async_copy(log_ref, log_hbm, sems.at[pairs + 2]),
+    ]
+    for copy in copies:
+        copy.start()
+
+    @pl.when(me_ref[0] != 0)
+    def _():
+        kv_heads = k_ref.shape[1] // HEAD_DIM
+        k2 = [block_diagonal(k_ref[:, kv * HEAD_DIM : (kv + 1) * HEAD_DIM]) for kv in range(kv_heads)]
+        late = [
+            grad_queries_of(pair, gs_ref, k2[pair * kv_heads // pairs], gq_ref, gq_hbm, sems.at[pair])
+            for pair in range(pairs)
+        ]
+        for copy in late:
+            copy.wait()
+
+    for copy in copies:
+        copy.wait()
 
 
 def local(queries, keys, values, grad_out, block_map, block_count):
@@ -193,35 +231,48 @@
         sent.reshape(cores * spans, 2 * rows, width), ("vis", "seq"), split_axis=0, concat_axis=0, tiled=True
     )
     pair_shape = (heads // 2, 2 * attended, tokens)
-    terms, grad_queries, log_totals = pl.pallas_call(
+    terms, grad_queries, logs, gs, k = pl.pallas_call(
         attend_kernel,
         out_shape=(
             shape((cores * travelling, width), BF16),
             shape(queries.shape, BF16),
             shape((heads, tokens), F32),
+            shape(pair_shape, BF16),
+            shape((attended, width), BF16),
         ),
-        in_specs=[VMEM] * 5,
-        out_specs=(VMEM, HBM, HBM),
-        scratch_shapes=[pltpu.VMEM(pair_shape, kind) for kind in (F32, F32, F32, BF16, BF16)]
+        in_specs=[SMEM] + [VMEM] * 5,
+        out_specs=(VMEM, HBM, VMEM, VMEM, VMEM),
+        scratch_shapes=[pltpu.VMEM(pair_shape, kind) for kind in (F32, F32, F32, BF16)]
         + [
             pltpu.VMEM(queries.shape, BF16),
-            pltpu.VMEM((heads, tokens), F32),
-            pltpu.SemaphoreType.DMA((heads // 2 + 1,)),
+            pltpu.SemaphoreType.DMA((heads // 2,)),
         ],
         compiler_params=params,
         name="attend",
-    )(q, g, order, live, got.reshape(-1, width))
+    )(me, q, g, order, live, got.reshape(-1, width))
     back = lax.all_to_all(
         terms.reshape(cores * spans, 2 * rows, width), ("vis", "seq"), split_axis=0, concat_axis=0, tiled=True
     )
-    grad_keys, grad_values = pl.pallas_call(
+    grad_keys, grad_values, log_totals, grad_queries = pl.pallas_call(
         functools.partial(sum_kernel, width, starts),
-        out_shape=(shape(keys.shape, BF16),) * 2,
-        in_specs=[VMEM, VMEM],
-        out_specs=(VMEM, VMEM),
+        out_shape=(
+            shape(keys.shape, BF16),
+            shape(keys.shape, BF16),
+            shape((heads, tokens), F32),
+            shape(queries.shape, BF16),
+        ),
+        in_specs=[SMEM] + [VMEM] * 5 + [HBM],
+        out_specs=(HBM,) * 4,
+        scratch_shapes=[
+            pltpu.VMEM(keys.shape, BF16),
+            pltpu.VMEM(keys.shape, BF16),
+            pltpu.VMEM(queries.shape, BF16),
+            pltpu.SemaphoreType.DMA((heads // 2 + 3,)),
+        ],
+        input_output_aliases={6: 3},
         compiler_params=params,
         name="sum_blocks",
-    )(pick, back.reshape(cores, -1, width))
+    )(me, pick, back.reshape(cores, -1, width), gs, k, logs, grad_queries)
     return grad_queries, log_totals, grad_keys, grad_values
 
 

time: 30.3 us -> 30.2 us (level)
  no operation moved by 1% of the time
where the time goes in v4:
time: 30.2 us; the launch traced here: 30 us
  blocking collectives  24.6 us (81%)
  Pallas kernels  4.68 us (15%)
  between operations  0.65 us (2%)
    all_to_all x1, blocking collectives, local(): lax.all_to_all(sent.reshape(cores * spans, 2 * rows, width), ('vis', 'seq...  15 us
    all_to_all x1, blocking collectives, local(): lax.all_to_all(terms.reshape(cores * spans, 2 * rows, width), ('vis', 'se...  9.62 us
    pallas_call x1, Pallas kernels, local(): pl.pallas_call(attend_kernel, out_shape=(shape((cores * travelling, width...  2.17 us
    pallas_call x1, Pallas kernels, local(): pl.pallas_call(functools.partial(choose_kernel, width, starts), out_shape...  1.66 us
    pallas_call x1, Pallas kernels, local(): pl.pallas_call(functools.partial(sum_kernel, width, starts), out_shape=(s...  0.85 us

profile of v4, /device:TPU:0, one launch (start us, length us, event | category | flops | bytes accessed | tf_op | source)
XLA Modules:
  0.0 30.0 jit_solution(18136604174536542199)
XLA Ops:
  0.6 1.7 %choose_blocks.1 = (bf16[2,128,256]{2,1,0:T(8,128)(2,1)S(1)}, bf16[32,128]{1,0:T(8,128)(2,1)S(1)}, bf16[128,256]{1,0:T(8,128)(2,1)S(1)}, f32[64,256]{1,0:T(8,128...) custom-call(s32[1]{0:T(128)} %bitcast.me_ref, s32[8,16]{1,0:T(8,128)} %bitcast.11, s32[1,16]{1,0:T(1,128)} %bitcast.12, ...), custom_call_target="tpu_custom_call" | custom-call | tf_op jit(solution)/shard_map/choose_blocks/pallas_call | solution.py:208
  2.3 15.0 %all_to_all.10 = bf16[32,8,256]{2,1,0:T(8,128)(2,1)S(1)} all-to-all(bf16[32,8,256]{2,1,0:T(8,128)(2,1)S(1)} %bitcast.10), channel_id=1, replica_groups=mesh['seq'=16,'vis'=2] {'vis','seq'}, dimensions={0} | all-to-all | bytes 262144 | tf_op jit(solution)/shard_map/all_to_all | solution.py:230
  17.3 2.2 %attend.1 = (bf16[256,256]{1,0:T(8,128)(2,1)S(1)}, bf16[256,2048]{1,0:T(8,128)(2,1)}, f32[16,256]{1,0:T(8,128)S(1)}, bf16[8,128,256]{2,1,0:T(8,128)(2,1)S(1)}, bf16[64,256]{1,0:T(8,128)(2,1)S(1)}) custom-call(s32[1]{0:T(128)} %bitcast.me_ref, bf16[256,2048]{1,0:T(8,128)(2,1)S(1)} %get-tuple-element.20.refs_0_, ...), custom_call_target="tpu_custom_call" | custom-call | tf_op jit(solution)/shard_map/attend/pallas_call | solution.py:234
  19.5 9.6 %all_to_all.11 = bf16[32,8,256]{2,1,0:T(8,128)(2,1)S(1)} all-to-all(bf16[32,8,256]{2,1,0:T(8,128)(2,1)S(1)} %bitcast.9), channel_id=1, replica_groups=mesh['seq'=16,'vis'=2] {'vis','seq'}, dimensions={0} | all-to-all | bytes 262144 | tf_op jit(solution)/shard_map/all_to_all | solution.py:253
  29.1 0.8 %sum_blocks.1 = (bf16[4,4,512]{2,1,0:T(4,128)(2,1)}, bf16[4,4,512]{2,1,0:T(4,128)(2,1)}, f32[16,256]{1,0:T(8,128)}, bf16[256,2048]{1,0:T(8,128)(2,1)}) custom-call(s32[1]{0:T(128)} %bitcast.me_ref, bf16[32,128]{1,0:T(8,128)(2,1)S(1)} %get-tuple-element.19.pick_ref, bf16[2,128,256]{2,1,0:T(8,128)(2,1)S(1)} %bitcast.8, ...), custom_call_target="tpu_custom_call", output_to_operand_aliasing={{3}: (6, {})} | custom-call | tf_op jit(solution)/shard_map/sum_blocks/pallas_call | solution.py:256

commit v5 on v4

--- a/solution.py
+++ b/solution.py
@@ -3,6 +3,7 @@
 
 import jax
 import jax.numpy as jnp
+import numpy as np
 from jax import lax
 from jax.experimental import pallas as pl
 from jax.experimental.pallas import tpu as pltpu
@@ -16,6 +17,19 @@
 VMEM = pl.BlockSpec(memory_space=pltpu.VMEM)
 HBM = pl.BlockSpec(memory_space=pltpu.HBM)
 SMEM = pl.BlockSpec(memory_space=pltpu.SMEM)
+EXCHANGE_ORDER = {
+    (16, 2): [18, 27, 28, 3, 6, 21, 13, 15, 22, 4, 12, 30, 7, 16, 23, 14, 20, 9, 17, 10, 29, 11, 0, 19, 26, 2, 24, 5, 1, 8, 31, 25],
+}
+
+
+def exchange_order(spans, cores):
+    return EXCHANGE_ORDER.get((spans, cores)) or [span * cores + core for core in range(cores) for span in range(spans)]
+
+
+def exchange(parts, order):
+    return lax.all_to_all(
+        parts, ("seq", "vis"), split_axis=0, concat_axis=0, tiled=True, axis_index_groups=[list(order)]
+    )
 
 
 def iota(shape, dim):
@@ -29,11 +43,11 @@
 
 
 def choose_kernel(
-    width, starts, me_ref, map_hbm, count_hbm, keys_hbm, values_hbm, q_hbm, g_hbm,
-    out_ref, pick_ref, order_ref, live_ref, q_ref, g_ref, map_ref, count_ref, keys_ref, values_ref, sems
+    starts, me_ref, map_hbm, count_hbm, place_hbm, keys_hbm, values_hbm, q_hbm, g_hbm,
+    out_ref, pick_ref, order_ref, live_ref, q_ref, g_ref, map_ref, count_ref, place_ref, keys_ref, values_ref, sems
 ):
     pairs = (
-        (map_hbm, map_ref), (count_hbm, count_ref), (keys_hbm, keys_ref), (values_hbm, values_ref), (q_hbm, q_ref), (g_hbm, g_ref)
+        (map_hbm, map_ref), (count_hbm, count_ref), (place_hbm, place_ref), (keys_hbm, keys_ref), (values_hbm, values_ref), (q_hbm, q_ref), (g_hbm, g_ref)
     )
     copies = [pltpu.make_async_copy(src, dst, sems.at[i]) for i, (src, dst) in enumerate(pairs)]
     for copy in copies:
@@ -43,43 +57,48 @@
     most, spans = map_ref.shape
     cores = len(starts)
 
-    slot_rows, span_rows = pick_ref.shape
-    expand_spans = (iota((span_rows, spans), 0) // (2 * rows) == iota((span_rows, spans), 1)).astype(BF16)
-    have, place = iota((slot_rows, 1), 0), iota((1, span_rows), 1) % (2 * rows)
+    _, slot_rows, travelling = pick_ref.shape
+    width = out_ref.shape[1]
+    have, part = iota((slot_rows, 1), 0), iota((1, travelling), 1) % (2 * rows)
     have_slot = (have % (per_owner * rows) // rows + 1).astype(F32)
-    have_place = have // (per_owner * rows) * rows + have % rows
-    same_place = have_place == place
+    same_part = have // (per_owner * rows) * rows + have % rows == part
 
     block_rows = cores * rows
     keys = most * block_rows
-    mine, theirs = iota((2 * keys, 1), 0), iota(order_ref.shape, 1)
+    mine = iota((2 * keys, 1), 0)
     block = mine % keys // block_rows
     expand_blocks = (iota((2 * keys, most), 1) == block).astype(BF16)
-    offset = mine % block_rows // rows * (spans * 2 * rows) + mine // keys * rows + mine % rows
+    same_row = mine // keys * rows + mine % rows == part
+    core = mine % block_rows // rows
     here = iota((1, spans), 1) == me
     live_block = iota(live_ref.shape, 0) // block_rows
 
-    for copy in copies[:4]:
+    for copy in copies[:5]:
         copy.wait()
     relative = map_ref[...] - me * per_owner
     asked = (relative >= 0) & (relative < per_owner) & (iota((most, spans), 0) < count_ref[...])
     slot = jnp.sum(jnp.where(asked, relative + 1, 0), axis=0, keepdims=True).astype(F32)
-    want = dot(jnp.broadcast_to(slot, (slot_rows, spans)).astype(BF16), expand_spans, 1, 1)
-    pick = ((want == have_slot) & same_place).astype(BF16)
+    place_span, place_core = place_ref[0:1, :], place_ref[1:2, :]
+    expand_spans = (iota((spans, travelling), 0) == place_span).astype(BF16)
+    want = dot(jnp.broadcast_to(slot, (slot_rows, spans)).astype(BF16), expand_spans)
+    asked = (want == have_slot) & same_part
     stacked = [ref[slot].astype(F32) for ref in (keys_ref, values_ref) for slot in range(per_owner)]
     stacked = jnp.concatenate(stacked, axis=0).astype(BF16)
-    for core, start in enumerate(starts):
-        out_ref[core] = dot(pick, stacked[:, start : start + width], 0, 0).astype(BF16)
-    pick_ref[...] = pick
+    out = 0.0
+    for to, start in enumerate(starts):
+        pick = (asked & (place_core == to)).astype(BF16)
+        pick_ref[to] = pick
+        out += dot(pick, stacked[:, start : start + width], 0, 0)
+    out_ref[...] = out.astype(BF16)
 
     owners = jnp.sum(jnp.where(here, map_ref[...] // per_owner, 0), axis=1, keepdims=True)
     count = jnp.sum(jnp.where(here, count_ref[...], 0), axis=1, keepdims=True)
-    lanes = jnp.broadcast_to(owners.astype(F32), (most, order_ref.shape[1])).astype(BF16)
+    lanes = jnp.broadcast_to(owners.astype(F32), (most, travelling)).astype(BF16)
     owner = dot(expand_blocks, lanes).astype(jnp.int32)
-    travels = jnp.where(block < count, offset, -theirs.shape[1] * most * spans) + owner * (2 * rows)
-    order_ref[...] = (travels == theirs).astype(BF16)
+    order = same_row & (owner == place_span) & (core == place_core) & (block < count)
+    order_ref[...] = order.astype(BF16)
     live_ref[...] = jnp.where(live_block < count, 0.0, -1e30)
-    for copy in copies[4:]:
+    for copy in copies[5:]:
         copy.wait()
 
 
@@ -154,13 +173,14 @@
 
 
 def sum_kernel(
-    width, starts, me_ref, pick_ref, terms_ref, gs_ref, k_ref, log_ref, _, keys_hbm, values_hbm, log_hbm, gq_hbm,
+    starts, me_ref, pick_ref, terms_ref, gs_ref, k_ref, log_ref, _, keys_hbm, values_hbm, log_hbm, gq_hbm,
     keys_ref, values_ref, gq_ref, sems
 ):
     per_owner, rows, _ = keys_ref.shape
+    width = terms_ref.shape[1]
     done = {}
     for core, start in enumerate(starts):
-        part = dot(pick_ref[...], terms_ref[core])
+        part = dot(pick_ref[core], terms_ref[...])
         done[start] = done[start] + part if start in done else part
     for start, total in done.items():
         for slot in range(per_owner):
@@ -200,41 +220,42 @@
     width = max(heads // GROUP, 1) * HEAD_DIM
     starts = tuple(core * heads // GROUP * HEAD_DIM for core in range(cores))
     attended = most * cores * rows
-    travelling = spans * 2 * rows
+    travelling = cores * spans * 2 * rows
+    order_of = exchange_order(spans, cores)
+    places = jnp.asarray(np.repeat(np.divmod(np.array(order_of, np.int32), cores), 2 * rows, axis=1))
     shape = jax.ShapeDtypeStruct
     params = pltpu.CompilerParams(vmem_limit_bytes=24 * 1024 * 1024)
     stay = functools.partial(pltpu.with_memory_space_constraint, memory_space=pltpu.HBM)
 
     sent, pick, order, live, q, g = pl.pallas_call(
-        functools.partial(choose_kernel, width, starts),
+        functools.partial(choose_kernel, starts),
         out_shape=(
-            shape((cores, travelling, width), BF16),
-            shape((2 * per_owner * rows, travelling), BF16),
-            shape((2 * attended, cores * travelling), BF16),
+            shape((travelling, width), BF16),
+            shape((cores, 2 * per_owner * rows, travelling), BF16),
+            shape((2 * attended, travelling), BF16),
             shape((attended, tokens), F32),
             shape(queries.shape, BF16),
             shape(queries.shape, BF16),
         ),
-        in_specs=[SMEM] + [HBM] * 6,
+        in_specs=[SMEM] + [HBM] * 7,
         out_specs=(VMEM,) * 6,
         scratch_shapes=[
             pltpu.VMEM((most, spans), jnp.int32),
             pltpu.VMEM((1, spans), jnp.int32),
+            pltpu.VMEM(places.shape, jnp.int32),
             pltpu.VMEM(keys.shape, BF16),
             pltpu.VMEM(keys.shape, BF16),
-            pltpu.SemaphoreType.DMA((6,)),
+            pltpu.SemaphoreType.DMA((7,)),
         ],
         compiler_params=params,
         name="choose_blocks",
-    )(me, *map(stay, (block_map.T, block_count.reshape(1, spans), keys, values, queries, grad_out)))
-    got = lax.all_to_all(
-        sent.reshape(cores * spans, 2 * rows, width), ("vis", "seq"), split_axis=0, concat_axis=0, tiled=True
-    )
+    )(me, *map(stay, (block_map.T, block_count.reshape(1, spans), places, keys, values, queries, grad_out)))
+    got = exchange(sent.reshape(cores * spans, 2 * rows, width), order_of)
     pair_shape = (heads // 2, 2 * attended, tokens)
     terms, grad_queries, logs, gs, k = pl.pallas_call(
         attend_kernel,
         out_shape=(
-            shape((cores * travelling, width), BF16),
+            shape((travelling, width), BF16),
             shape(queries.shape, BF16),
             shape((heads, tokens), F32),
             shape(pair_shape, BF16),
@@ -250,11 +271,9 @@
         compiler_params=params,
         name="attend",
     )(me, q, g, order, live, got.reshape(-1, width))
-    back = lax.all_to_all(
-        terms.reshape(cores * spans, 2 * rows, width), ("vis", "seq"), split_axis=0, concat_axis=0, tiled=True
-    )
+    back = exchange(terms.reshape(cores * spans, 2 * rows, width), order_of)
     grad_keys, grad_values, log_totals, grad_queries = pl.pallas_call(
-        functools.partial(sum_kernel, width, starts),
+        functools.partial(sum_kernel, starts),
         out_shape=(
             shape(keys.shape, BF16),
             shape(keys.shape, BF16),
@@ -272,7 +291,7 @@
         input_output_aliases={6: 3},
         compiler_params=params,
         name="sum_blocks",
-    )(me, pick, back.reshape(cores, -1, width), gs, k, logs, grad_queries)
+    )(me, pick, back.reshape(-1, width), gs, k, logs, grad_queries)
     return grad_queries, log_totals, grad_keys, grad_values
 
 

time: 30.2 us -> 29.2 us (0.967)
  blocking collectives: 24.6 us -> 23.6 us
    all_to_all x2, blocking collectives: 24.6 us -> 23.6 us  [exchange(): lax.all_to_all(parts, ('seq', 'vis'), split_axis=0, concat_axis=0, tiled=...]
where the time goes in v5:
time: 29.2 us; the launch traced here: 29 us
  blocking collectives  23.6 us (81%)
  Pallas kernels  4.69 us (16%)
  between operations  0.65 us (2%)
    all_to_all x2, blocking collectives, exchange(): lax.all_to_all(parts, ('seq', 'vis'), split_axis=0, concat_axis=0, tiled=...  23.6 us
    pallas_call x1, Pallas kernels, local(): pl.pallas_call(attend_kernel, out_shape=(shape((travelling, width), BF16)...  2.14 us
    pallas_call x1, Pallas kernels, local(): pl.pallas_call(functools.partial(choose_kernel, starts), out_shape=(shape...  1.69 us
    pallas_call x1, Pallas kernels, local(): pl.pallas_call(functools.partial(sum_kernel, starts), out_shape=(shape(ke...  0.87 us

profile of v5, /device:TPU:0, one launch (start us, length us, event | category | flops | bytes accessed | tf_op | source)
XLA Modules:
  0.0 29.0 jit_solution(8599272550271229341)
XLA Ops:
  0.6 1.7 %choose_blocks.1 = (bf16[256,256]{1,0:T(8,128)(2,1)S(1)}, bf16[2,32,256]{2,1,0:T(8,128)(2,1)S(1)}, bf16[128,256]{1,0:T(8,128)(2,1)S(1)}, f32[64,256]{1,0:T(8,128...) custom-call(s32[1]{0:T(128)} %bitcast.me_ref, s32[8,16]{1,0:T(8,128)} %bitcast.11, s32[1,16]{1,0:T(1,128)} %bitcast.12, ...), custom_call_target="tpu_custom_call" | custom-call | tf_op jit(solution)/shard_map/choose_blocks/pallas_call | solution.py:230
  2.3 14.4 %all_to_all.10 = bf16[32,8,256]{2,1,0:T(8,128)(2,1)S(1)} all-to-all(bf16[32,8,256]{2,1,0:T(8,128)(2,1)S(1)} %bitcast.10), channel_id=1, replica_groups={{18,27,28,3,6,21,13,15,22,4,12,30,7,16,23,14,20,9,17,10,29,11,0,19,26,2..., dimensions={0} | all-to-all | bytes 262144 | tf_op jit(solution)/shard_map/all_to_all | solution.py:30
  16.7 2.1 %attend.1 = (bf16[256,256]{1,0:T(8,128)(2,1)S(1)}, bf16[256,2048]{1,0:T(8,128)(2,1)}, f32[16,256]{1,0:T(8,128)S(1)}, bf16[8,128,256]{2,1,0:T(8,128)(2,1)S(1)}, bf16[64,256]{1,0:T(8,128)(2,1)S(1)}) custom-call(s32[1]{0:T(128)} %bitcast.me_ref, bf16[256,2048]{1,0:T(8,128)(2,1)S(1)} %get-tuple-element.20.refs_0_, ...), custom_call_target="tpu_custom_call" | custom-call | tf_op jit(solution)/shard_map/attend/pallas_call | solution.py:255
  18.8 9.3 %all_to_all.11 = bf16[32,8,256]{2,1,0:T(8,128)(2,1)S(1)} all-to-all(bf16[32,8,256]{2,1,0:T(8,128)(2,1)S(1)} %bitcast.9), channel_id=1, replica_groups={{18,27,28,3,6,21,13,15,22,4,12,30,7,16,23,14,20,9,17,10,29,11,0,19,26,2..., dimensions={0} | all-to-all | bytes 262144 | tf_op jit(solution)/shard_map/all_to_all | solution.py:30
  28.1 0.9 %sum_blocks.1 = (bf16[4,4,512]{2,1,0:T(4,128)(2,1)}, bf16[4,4,512]{2,1,0:T(4,128)(2,1)}, f32[16,256]{1,0:T(8,128)}, bf16[256,2048]{1,0:T(8,128)(2,1)}) custom-call(s32[1]{0:T(128)} %bitcast.me_ref, bf16[2,32,256]{2,1,0:T(8,128)(2,1)S(1)} %get-tuple-element.19.pick_ref, bf16[256,256]{1,0:T(8,128)(2,1)S(1)} %bitcast.8, ...), custom_call_target="tpu_custom_call", output_to_operand_aliasing={{3}: (6, {})} | custom-call | tf_op jit(solution)/shard_map/sum_blocks/pallas_call | solution.py:275

commit v6 on v5

--- a/solution.py
+++ b/solution.py
@@ -43,11 +43,11 @@
 
 
 def choose_kernel(
-    starts, me_ref, map_hbm, count_hbm, place_hbm, keys_hbm, values_hbm, q_hbm, g_hbm,
-    out_ref, pick_ref, order_ref, live_ref, q_ref, g_ref, map_ref, count_ref, place_ref, keys_ref, values_ref, sems
+    starts, me_ref, map_hbm, count_hbm, place_hbm, keys_hbm, values_hbm,
+    out_ref, pick_ref, order_ref, live_ref, map_ref, count_ref, place_ref, keys_ref, values_ref, sems
 ):
     pairs = (
-        (map_hbm, map_ref), (count_hbm, count_ref), (place_hbm, place_ref), (keys_hbm, keys_ref), (values_hbm, values_ref), (q_hbm, q_ref), (g_hbm, g_ref)
+        (map_hbm, map_ref), (count_hbm, count_ref), (place_hbm, place_ref), (keys_hbm, keys_ref), (values_hbm, values_ref)
     )
     copies = [pltpu.make_async_copy(src, dst, sems.at[i]) for i, (src, dst) in enumerate(pairs)]
     for copy in copies:
@@ -73,7 +73,7 @@
     here = iota((1, spans), 1) == me
     live_block = iota(live_ref.shape, 0) // block_rows
 
-    for copy in copies[:5]:
+    for copy in copies:
         copy.wait()
     relative = map_ref[...] - me * per_owner
     asked = (relative >= 0) & (relative < per_owner) & (iota((most, spans), 0) < count_ref[...])
@@ -98,8 +98,6 @@
     order = same_row & (owner == place_span) & (core == place_core) & (block < count)
     order_ref[...] = order.astype(BF16)
     live_ref[...] = jnp.where(live_block < count, 0.0, -1e30)
-    for copy in copies[5:]:
-        copy.wait()
 
 
 def block_diagonal(part):
@@ -133,9 +131,13 @@
     k2 = [block_diagonal(head[:keys]) for head in heads for _ in range(pairs // kv_heads)]
     v2 = [block_diagonal(head[keys:]) for head in heads for _ in range(pairs // kv_heads)]
 
-    for pair, at in enumerate(columns):
-        scores_ref[pair] = dot(k2[pair], q_ref[:, at], 1, 1)
-    for pair in range(pairs):
+    copies = []
+    gk, gv = [0.0] * kv_heads, [0.0] * kv_heads
+
+    def score(pair):
+        scores_ref[pair] = dot(k2[pair], q_ref[:, columns[pair]], 1, 1)
+
+    def soften(pair):
         scores = scores_ref[pair].reshape(split) * (score_scale * LOG2E) + live
         row_max = jnp.max(scores, axis=1, keepdims=True)
         weights = jnp.exp2(scores - row_max)
@@ -144,21 +146,37 @@
         log_ref[2 * pair : 2 * pair + 2, :] = ((row_max + jnp.log2(totals)) * (1.0 / LOG2E)).reshape(2, tokens)
         probs_ref[pair] = probs.reshape(joined)
         low_ref[pair] = probs.astype(BF16).reshape(joined)
-    copies = []
-    for pair, at in enumerate(columns):
-        gp_ref[pair] = dot(v2[pair], g_ref[:, at], 1, 1)
-    for pair in range(pairs):
+
+    def against_values(pair):
+        gp_ref[pair] = dot(v2[pair], g_ref[:, columns[pair]], 1, 1)
+
+    def grad_score(pair):
         grad_probs = gp_ref[pair].reshape(split)
         delta = jnp.sum(low_ref[pair].reshape(split).astype(F32) * grad_probs, axis=1, keepdims=True)
         gs_ref[pair] = (probs_ref[pair].reshape(split) * (grad_probs - delta)).astype(BF16).reshape(joined)
-    if early:
-        for pair in range(pairs):
+
+    def add_values(pair):
+        gv[pair * kv_heads // pairs] += dot(low_ref[pair], g_ref[:, columns[pair]])
+
+    def add_keys(pair):
+        gk[pair * kv_heads // pairs] += dot(gs_ref[pair], q_ref[:, columns[pair]])
+
+    def add_queries(pair):
+        if early:
             copies.append(grad_queries_of(pair, gs_ref, k2[pair], gq_ref, gq_hbm, sems.at[pair]))
-    gk, gv = [0.0] * kv_heads, [0.0] * kv_heads
-    for pair, at in enumerate(columns):
-        kv = pair * kv_heads // pairs
-        gk[kv] += dot(gs_ref[pair], q_ref[:, at])
-        gv[kv] += dot(low_ref[pair], g_ref[:, at])
+
+    for pair in range(pairs):
+        score(pair)
+        against_values(pair)
+    for pair in range(pairs):
+        soften(pair)
+    for pair in range(pairs):
+        grad_score(pair)
+        add_values(pair)
+    for pair in range(pairs):
+        add_queries(pair)
+    for pair in range(pairs):
+        add_keys(pair)
     gk = [(part[:keys, :HEAD_DIM] + part[keys:, HEAD_DIM:]) * score_scale for part in gk]
     gv = [part[:keys, :HEAD_DIM] + part[keys:, HEAD_DIM:] for part in gv]
     terms = jnp.concatenate([jnp.concatenate(gk, 1), jnp.concatenate(gv, 1)], 0).astype(BF16)
@@ -227,29 +245,28 @@
     params = pltpu.CompilerParams(vmem_limit_bytes=24 * 1024 * 1024)
     stay = functools.partial(pltpu.with_memory_space_constraint, memory_space=pltpu.HBM)
 
-    sent, pick, order, live, q, g = pl.pallas_call(
+    sent, pick, order, live = pl.pallas_call(
         functools.partial(choose_kernel, starts),
         out_shape=(
             shape((travelling, width), BF16),
             shape((cores, 2 * per_owner * rows, travelling), BF16),
             shape((2 * attended, travelling), BF16),
             shape((attended, tokens), F32),
-            shape(queries.shape, BF16),
-            shape(queries.shape, BF16),
         ),
-        in_specs=[SMEM] + [HBM] * 7,
-        out_specs=(VMEM,) * 6,
+        in_specs=[SMEM] + [HBM] * 5,
+        out_specs=(VMEM,) * 4,
         scratch_shapes=[
             pltpu.VMEM((most, spans), jnp.int32),
             pltpu.VMEM((1, spans), jnp.int32),
             pltpu.VMEM(places.shape, jnp.int32),
             pltpu.VMEM(keys.shape, BF16),
             pltpu.VMEM(keys.shape, BF16),
-            pltpu.SemaphoreType.DMA((7,)),
+            pltpu.SemaphoreType.DMA((5,)),
         ],
         compiler_params=params,
+        cost_estimate=pl.CostEstimate(flops=10**10, bytes_accessed=10**6, transcendentals=0),
         name="choose_blocks",
-    )(me, *map(stay, (block_map.T, block_count.reshape(1, spans), places, keys, values, queries, grad_out)))
+    )(me, *map(stay, (block_map.T, block_count.reshape(1, spans), places, keys, values)))
     got = exchange(sent.reshape(cores * spans, 2 * rows, width), order_of)
     pair_shape = (heads // 2, 2 * attended, tokens)
     terms, grad_queries, logs, gs, k = pl.pallas_call(
@@ -270,7 +287,7 @@
         ],
         compiler_params=params,
         name="attend",
-    )(me, q, g, order, live, got.reshape(-1, width))
+    )(me, queries, grad_out, order, live, got.reshape(-1, width))
     back = exchange(terms.reshape(cores * spans, 2 * rows, width), order_of)
     grad_keys, grad_values, log_totals, grad_queries = pl.pallas_call(
         functools.partial(sum_kernel, starts),

time: 29.2 us -> 28.9 us (0.990)
  blocking collectives: 23.6 us -> 23.3 us
    all_to_all x2, blocking collectives: 23.6 us -> 23.3 us  [exchange(): lax.all_to_all(parts, ('seq', 'vis'), split_axis=0, concat_axis=0, tiled=...]
where the time goes in v6:
time: 28.9 us; the launch traced here: 28.6 us
  blocking collectives  23.3 us (81%)
  Pallas kernels  4.59 us (16%)
  between operations  0.67 us (2%)
    all_to_all x2, blocking collectives, exchange(): lax.all_to_all(parts, ('seq', 'vis'), split_axis=0, concat_axis=0, tiled=...  23.3 us
    pallas_call x1, Pallas kernels, local(): pl.pallas_call(attend_kernel, out_shape=(shape((travelling, width), BF16)...  2.32 us
    pallas_call x1, Pallas kernels, local(): pl.pallas_call(functools.partial(choose_kernel, starts), out_shape=(shape...  1.41 us
    pallas_call x1, Pallas kernels, local(): pl.pallas_call(functools.partial(sum_kernel, starts), out_shape=(shape(ke...  0.87 us

profile of v6, /device:TPU:0, one launch (start us, length us, event | category | flops | bytes accessed | tf_op | source)
XLA Modules:
  0.0 28.6 jit_solution(6634054159249989799)
XLA Ops:
  0.6 0.0 copy-start
  0.6 0.0 copy-start.1
  0.7 1.4 %choose_blocks.1 = (bf16[256,256]{1,0:T(8,128)(2,1)S(1)}, bf16[2,32,256]{2,1,0:T(8,128)(2,1)S(1)}, bf16[128,256]{1,0:T(8,128)(2,1)S(1)}, f32[64,256]{1,0:T(8,128)S(1)}) custom-call(s32[1]{0:T(128)} %bitcast.me_ref, s32[8,16]{1,0:T(8,128)} %bitcast.11, s32[1,16]{1,0:T(1,128)} %bitcast.12, s32[2,256]{1,0:T(2,128)} %constant.8.clone.place_hbm, ...), custom_call_target="tpu_custom_call" | custom-call | flops 10000000000 | bytes 1000000 | tf_op jit(solution)/shard_map/choose_blocks/pallas_call | solution.py:248
  2.1 14.4 %all_to_all.10 = bf16[32,8,256]{2,1,0:T(8,128)(2,1)S(1)} all-to-all(bf16[32,8,256]{2,1,0:T(8,128)(2,1)S(1)} %bitcast.10), channel_id=1, replica_groups={{18,27,28,3,6,21,13,15,22,4,12,30,7,16,23,14,20,9,17,10,29,11,0,19,26,2..., dimensions={0} | all-to-all | bytes 262144 | tf_op jit(solution)/shard_map/all_to_all | solution.py:30
  16.4 0.0 copy-done
  16.4 0.0 copy-done.1
  16.4 2.3 %attend.1 = (bf16[256,256]{1,0:T(8,128)(2,1)S(1)}, bf16[256,2048]{1,0:T(8,128)(2,1)}, f32[16,256]{1,0:T(8,128)S(1)}, bf16[8,128,256]{2,1,0:T(8,128)(2,1)S(1)}, bf16[64,256]{1,0:T(8,128)(2,1)S(1)}) custom-call(s32[1]{0:T(128)} %bitcast.me_ref, bf16[256,2048]{1,0:T(8,128)(2,1)S(1)} %copy-done, bf16[256,2048]{1,0:T(8,128)(2,1)S(1)} %copy-done.1, ...), custom_call_target="tpu_custom_call" | custom-call | tf_op jit(solution)/shard_map/attend/pallas_call | solution.py:272
  18.8 9.0 %all_to_all.11 = bf16[32,8,256]{2,1,0:T(8,128)(2,1)S(1)} all-to-all(bf16[32,8,256]{2,1,0:T(8,128)(2,1)S(1)} %bitcast.9), channel_id=1, replica_groups={{18,27,28,3,6,21,13,15,22,4,12,30,7,16,23,14,20,9,17,10,29,11,0,19,26,2..., dimensions={0} | all-to-all | bytes 262144 | tf_op jit(solution)/shard_map/all_to_all | solution.py:30
  27.7 0.9 %sum_blocks.1 = (bf16[4,4,512]{2,1,0:T(4,128)(2,1)}, bf16[4,4,512]{2,1,0:T(4,128)(2,1)}, f32[16,256]{1,0:T(8,128)}, bf16[256,2048]{1,0:T(8,128)(2,1)}) custom-call(s32[1]{0:T(128)} %bitcast.me_ref, bf16[2,32,256]{2,1,0:T(8,128)(2,1)S(1)} %get-tuple-element.17.pick_ref, bf16[256,256]{1,0:T(8,128)(2,1)S(1)} %bitcast.8, ...), custom_call_target="tpu_custom_call", output_to_operand_aliasing={{3}: (6, {})} | custom-call | tf_op jit(solution)/shard_map/sum_blocks/pallas_call | solution.py:292
Async XLA Ops:
  0.6 15.8 %copy-start = (bf16[256,2048]{1,0:T(8,128)(2,1)S(1)}, bf16[256,2048]{1,0:T(8,128)(2,1)}, u32[]{:S(2)}) copy-start(bf16[256,2048]{1,0:T(8,128)(2,1)} %refs_0_.1) | copy-start | bytes 3145732
  0.6 15.8 %copy-start.1 = (bf16[256,2048]{1,0:T(8,128)(2,1)S(1)}, bf16[256,2048]{1,0:T(8,128)(2,1)}, u32[]{:S(2)}) copy-start(bf16[256,2048]{1,0:T(8,128)(2,1)} %refs_1_.1) | copy-start | bytes 3145732

commit v7 on v6

--- a/solution.py
+++ b/solution.py
@@ -42,16 +42,18 @@
     )
 
 
+def load_kernel(*refs):
+    sems, half = refs[-1], len(refs) // 2
+    copies = [pltpu.make_async_copy(src, dst, sems.at[i]) for i, (src, dst) in enumerate(zip(refs[:half], refs[half:-1]))]
+    for copy in copies:
+        copy.start()
+    for copy in copies:
+        copy.wait()
+
+
 def choose_kernel(
-    starts, me_ref, map_hbm, count_hbm, place_hbm, keys_hbm, values_hbm,
-    out_ref, pick_ref, order_ref, live_ref, map_ref, count_ref, place_ref, keys_ref, values_ref, sems
+    starts, me_ref, map_ref, count_ref, place_ref, keys_ref, values_ref, out_ref, pick_ref, order_ref, live_ref
 ):
-    pairs = (
-        (map_hbm, map_ref), (count_hbm, count_ref), (place_hbm, place_ref), (keys_hbm, keys_ref), (values_hbm, values_ref)
-    )
-    copies = [pltpu.make_async_copy(src, dst, sems.at[i]) for i, (src, dst) in enumerate(pairs)]
-    for copy in copies:
-        copy.start()
     me = me_ref[0]
     per_owner, rows, _ = keys_ref.shape
     most, spans = map_ref.shape
@@ -73,14 +75,18 @@
     here = iota((1, spans), 1) == me
     live_block = iota(live_ref.shape, 0) // block_rows
 
-    for copy in copies:
-        copy.wait()
     relative = map_ref[...] - me * per_owner
     asked = (relative >= 0) & (relative < per_owner) & (iota((most, spans), 0) < count_ref[...])
     slot = jnp.sum(jnp.where(asked, relative + 1, 0), axis=0, keepdims=True).astype(F32)
     place_span, place_core = place_ref[0:1, :], place_ref[1:2, :]
-    expand_spans = (iota((spans, travelling), 0) == place_span).astype(BF16)
-    want = dot(jnp.broadcast_to(slot, (slot_rows, spans)).astype(BF16), expand_spans)
+    lanes = 128
+    slots = jnp.concatenate([slot, jnp.zeros((1, lanes - spans), F32)], axis=1)
+    slots = jnp.broadcast_to(slots, (8, lanes))
+    want = [
+        jnp.take_along_axis(slots, jnp.broadcast_to(place_span[:, at : at + lanes], (8, lanes)), axis=1, mode="promise_in_bounds")[:1]
+        for at in range(0, travelling, lanes)
+    ]
+    want = jnp.concatenate(want, axis=1)
     asked = (want == have_slot) & same_part
     stacked = [ref[slot].astype(F32) for ref in (keys_ref, values_ref) for slot in range(per_owner)]
     stacked = jnp.concatenate(stacked, axis=0).astype(BF16)
@@ -245,6 +251,16 @@
     params = pltpu.CompilerParams(vmem_limit_bytes=24 * 1024 * 1024)
     stay = functools.partial(pltpu.with_memory_space_constraint, memory_space=pltpu.HBM)
 
+    inputs = (block_map.T, block_count.reshape(1, spans), places, keys, values)
+    inputs = pl.pallas_call(
+        load_kernel,
+        out_shape=tuple(shape(part.shape, part.dtype) for part in inputs),
+        in_specs=[HBM] * 5,
+        out_specs=(VMEM,) * 5,
+        scratch_shapes=[pltpu.SemaphoreType.DMA((5,))],
+        compiler_params=params,
+        name="load_blocks",
+    )(*map(stay, inputs))
     sent, pick, order, live = pl.pallas_call(
         functools.partial(choose_kernel, starts),
         out_shape=(
@@ -253,20 +269,12 @@
             shape((2 * attended, travelling), BF16),
             shape((attended, tokens), F32),
         ),
-        in_specs=[SMEM] + [HBM] * 5,
+        in_specs=[SMEM] + [VMEM] * 5,
         out_specs=(VMEM,) * 4,
-        scratch_shapes=[
-            pltpu.VMEM((most, spans), jnp.int32),
-            pltpu.VMEM((1, spans), jnp.int32),
-            pltpu.VMEM(places.shape, jnp.int32),
-            pltpu.VMEM(keys.shape, BF16),
-            pltpu.VMEM(keys.shape, BF16),
-            pltpu.SemaphoreType.DMA((5,)),
-        ],
         compiler_params=params,
         cost_estimate=pl.CostEstimate(flops=10**10, bytes_accessed=10**6, transcendentals=0),
         name="choose_blocks",
-    )(me, *map(stay, (block_map.T, block_count.reshape(1, spans), places, keys, values)))
+    )(me, *inputs)
     got = exchange(sent.reshape(cores * spans, 2 * rows, width), order_of)
     pair_shape = (heads // 2, 2 * attended, tokens)
     terms, grad_queries, logs, gs, k = pl.pallas_call(

time: 28.9 us -> 28.7 us (level)
    pallas_call x1, Pallas kernels: 1.41 us -> 0.39 us  [local(): pl.pallas_call(functools.partial(choose_kernel, starts), out_shape=(shape...]
    pallas_call x0 -> x1, Pallas kernels: none -> 0.83 us  [local(): pl.pallas_call(load_kernel, out_shape=tuple((shape(part.shape, part.dtype...]
where the time goes in v7:
time: 28.7 us; the launch traced here: 28.4 us
  blocking collectives  23.3 us (81%)
  Pallas kernels  4.39 us (15%)
  between operations  0.68 us (2%)
    all_to_all x2, blocking collectives, exchange(): lax.all_to_all(parts, ('seq', 'vis'), split_axis=0, concat_axis=0, tiled=...  23.3 us
    pallas_call x1, Pallas kernels, local(): pl.pallas_call(attend_kernel, out_shape=(shape((travelling, width), BF16)...  2.3 us
    pallas_call x1, Pallas kernels, local(): pl.pallas_call(functools.partial(sum_kernel, starts), out_shape=(shape(ke...  0.87 us
    pallas_call x1, Pallas kernels, local(): pl.pallas_call(load_kernel, out_shape=tuple((shape(part.shape, part.dtype...  0.83 us

profile of v7, /device:TPU:0, one launch (start us, length us, event | category | flops | bytes accessed | tf_op | source)
XLA Modules:
  0.0 28.4 jit_solution(13876877173694843181)
XLA Ops:
  0.6 0.8 %load_blocks.1 = (s32[8,16]{1,0:T(8,128)S(1)}, s32[1,16]{1,0:T(1,128)S(1)}, s32[2,256]{1,0:T(2,128)S(1)}, bf16[4,4,512]{2,1,0:T(4,128)(2,1)S(1)}, bf16[4,4,512]{2,1,0:T(4,128)(2,1)S(1)}) custom-call(s32[8,16]{1,0:T(8,128)} %bitcast.11, s32[1,16]{1,0:T(1,128)} %bitcast.12, s32[2,256]{1,0:T(2,128)} %constant.8.clone.refs_2_, bf16[4,4,512]{2,1,0:T(4,128)(2,1)} %refs_3_.1, ...), custom_call_target="tpu_custom_call" | custom-call | tf_op jit(solution)/shard_map/load_blocks/pallas_call | solution.py:255
  1.5 0.0 copy-start
  1.5 0.0 copy-start.1
  1.5 0.4 %choose_blocks.1 = (bf16[256,256]{1,0:T(8,128)(2,1)S(1)}, bf16[2,32,256]{2,1,0:T(8,128)(2,1)S(1)}, bf16[128,256]{1,0:T(8,128)(2,1)S(1)}, f32[64,256]{1,0:T(8,128)S(1)}) custom-call(s32[1]{0:T(128)} %bitcast.me_ref, s32[8,16]{1,0:T(8,128)S(1)} %get-tuple-element.22.map_ref, s32[1,16]{1,0:T(1,128)S(1)} %get-tuple-element.23.count_ref, ...), custom_call_target="tpu_custom_call" | custom-call | flops 10000000000 | bytes 1000000 | tf_op jit(solution)/shard_map/choose_blocks/pallas_call | solution.py:264
  1.9 14.4 %all_to_all.10 = bf16[32,8,256]{2,1,0:T(8,128)(2,1)S(1)} all-to-all(bf16[32,8,256]{2,1,0:T(8,128)(2,1)S(1)} %bitcast.9), channel_id=1, replica_groups={{18,27,28,3,6,21,13,15,22,4,12,30,7,16,23,14,20,9,17,10,29,11,0,19,26,2..., dimensions={0} | all-to-all | bytes 262144 | tf_op jit(solution)/shard_map/all_to_all | solution.py:30
  16.3 0.0 copy-done
  16.3 0.0 copy-done.1
  16.3 2.3 %attend.1 = (bf16[256,256]{1,0:T(8,128)(2,1)S(1)}, bf16[256,2048]{1,0:T(8,128)(2,1)}, f32[16,256]{1,0:T(8,128)S(1)}, bf16[8,128,256]{2,1,0:T(8,128)(2,1)S(1)}, bf16[64,256]{1,0:T(8,128)(2,1)S(1)}) custom-call(s32[1]{0:T(128)} %bitcast.me_ref, bf16[256,2048]{1,0:T(8,128)(2,1)S(1)} %copy-done, bf16[256,2048]{1,0:T(8,128)(2,1)S(1)} %copy-done.1, ...), custom_call_target="tpu_custom_call" | custom-call | tf_op jit(solution)/shard_map/attend/pallas_call | solution.py:280
  18.6 9.0 %all_to_all.11 = bf16[32,8,256]{2,1,0:T(8,128)(2,1)S(1)} all-to-all(bf16[32,8,256]{2,1,0:T(8,128)(2,1)S(1)} %bitcast.10), channel_id=1, replica_groups={{18,27,28,3,6,21,13,15,22,4,12,30,7,16,23,14,20,9,17,10,29,11,0,19,26,2..., dimensions={0} | all-to-all | bytes 262144 | tf_op jit(solution)/shard_map/all_to_all | solution.py:30
  27.6 0.9 %sum_blocks.1 = (bf16[4,4,512]{2,1,0:T(4,128)(2,1)}, bf16[4,4,512]{2,1,0:T(4,128)(2,1)}, f32[16,256]{1,0:T(8,128)}, bf16[256,2048]{1,0:T(8,128)(2,1)}) custom-call(s32[1]{0:T(128)} %bitcast.me_ref, bf16[2,32,256]{2,1,0:T(8,128)(2,1)S(1)} %get-tuple-element.27.pick_ref, bf16[256,256]{1,0:T(8,128)(2,1)S(1)} %bitcast.8, ...), custom_call_target="tpu_custom_call", output_to_operand_aliasing={{3}: (6, {})} | custom-call | tf_op jit(solution)/shard_map/sum_blocks/pallas_call | solution.py:300
Async XLA Ops:
  1.5 14.8 %copy-start = (bf16[256,2048]{1,0:T(8,128)(2,1)S(1)}, bf16[256,2048]{1,0:T(8,128)(2,1)}, u32[]{:S(2)}) copy-start(bf16[256,2048]{1,0:T(8,128)(2,1)} %refs_0_.1) | copy-start | bytes 3145732
  1.5 14.8 %copy-start.1 = (bf16[256,2048]{1,0:T(8,128)(2,1)S(1)}, bf16[256,2048]{1,0:T(8,128)(2,1)}, u32[]{:S(2)}) copy-start(bf16[256,2048]{1,0:T(8,128)(2,1)} %refs_1_.1) | copy-start | bytes 3145732

commit v8 on v7

--- a/solution.py
+++ b/solution.py
@@ -59,11 +59,14 @@
     most, spans = map_ref.shape
     cores = len(starts)
 
-    _, slot_rows, travelling = pick_ref.shape
+    pick_rows, travelling = pick_ref.shape
+    slot_rows = pick_rows // cores
     width = out_ref.shape[1]
-    have, part = iota((slot_rows, 1), 0), iota((1, travelling), 1) % (2 * rows)
+    place_span, place_core = place_ref[0:1, :], place_ref[1:2, :]
+    have, part = iota((pick_rows, 1), 0), iota((1, travelling), 1) % (2 * rows)
     have_slot = (have % (per_owner * rows) // rows + 1).astype(F32)
-    same_part = have // (per_owner * rows) * rows + have % rows == part
+    same_part = have % slot_rows // (per_owner * rows) * rows + have % rows == part
+    same_place = same_part & (have // slot_rows == place_core)
 
     block_rows = cores * rows
     keys = most * block_rows
@@ -78,7 +81,6 @@
     relative = map_ref[...] - me * per_owner
     asked = (relative >= 0) & (relative < per_owner) & (iota((most, spans), 0) < count_ref[...])
     slot = jnp.sum(jnp.where(asked, relative + 1, 0), axis=0, keepdims=True).astype(F32)
-    place_span, place_core = place_ref[0:1, :], place_ref[1:2, :]
     lanes = 128
     slots = jnp.concatenate([slot, jnp.zeros((1, lanes - spans), F32)], axis=1)
     slots = jnp.broadcast_to(slots, (8, lanes))
@@ -87,15 +89,12 @@
         for at in range(0, travelling, lanes)
     ]
     want = jnp.concatenate(want, axis=1)
-    asked = (want == have_slot) & same_part
+    pick = ((want == have_slot) & same_place).astype(BF16)
+    pick_ref[...] = pick
     stacked = [ref[slot].astype(F32) for ref in (keys_ref, values_ref) for slot in range(per_owner)]
     stacked = jnp.concatenate(stacked, axis=0).astype(BF16)
-    out = 0.0
-    for to, start in enumerate(starts):
-        pick = (asked & (place_core == to)).astype(BF16)
-        pick_ref[to] = pick
-        out += dot(pick, stacked[:, start : start + width], 0, 0)
-    out_ref[...] = out.astype(BF16)
+    stacked = jnp.concatenate([stacked[:, start : start + width] for start in starts], axis=0)
+    out_ref[...] = dot(pick, stacked, 0, 0).astype(BF16)
 
     owners = jnp.sum(jnp.where(here, map_ref[...] // per_owner, 0), axis=1, keepdims=True)
     count = jnp.sum(jnp.where(here, count_ref[...], 0), axis=1, keepdims=True)
@@ -202,9 +201,11 @@
 ):
     per_owner, rows, _ = keys_ref.shape
     width = terms_ref.shape[1]
+    totals = dot(pick_ref[...], terms_ref[...])
+    slot_rows = 2 * per_owner * rows
     done = {}
     for core, start in enumerate(starts):
-        part = dot(pick_ref[core], terms_ref[...])
+        part = totals[core * slot_rows : (core + 1) * slot_rows]
         done[start] = done[start] + part if start in done else part
     for start, total in done.items():
         for slot in range(per_owner):
@@ -265,7 +266,7 @@
         functools.partial(choose_kernel, starts),
         out_shape=(
             shape((travelling, width), BF16),
-            shape((cores, 2 * per_owner * rows, travelling), BF16),
+            shape((cores * 2 * per_owner * rows, travelling), BF16),
             shape((2 * attended, travelling), BF16),
             shape((attended, tokens), F32),
         ),

time: 28.7 us -> 28.7 us (level)
  no operation moved by 1% of the time
where the time goes in v8:
time: 28.7 us; the launch traced here: 28.4 us
  blocking collectives  23.3 us (81%)
  Pallas kernels  4.33 us (15%)
  between operations  0.68 us (2%)
    all_to_all x2, blocking collectives, exchange(): lax.all_to_all(parts, ('seq', 'vis'), split_axis=0, concat_axis=0, tiled=...  23.3 us
    pallas_call x1, Pallas kernels, local(): pl.pallas_call(attend_kernel, out_shape=(shape((travelling, width), BF16)...  2.3 us
    pallas_call x1, Pallas kernels, local(): pl.pallas_call(functools.partial(sum_kernel, starts), out_shape=(shape(ke...  0.87 us
    pallas_call x1, Pallas kernels, local(): pl.pallas_call(load_kernel, out_shape=tuple((shape(part.shape, part.dtype...  0.83 us

profile of v8, /device:TPU:0, one launch (start us, length us, event | category | flops | bytes accessed | tf_op | source)
XLA Modules:
  0.0 28.4 jit_solution(3856708701895389813)
XLA Ops:
  0.6 0.8 %load_blocks.1 = (s32[8,16]{1,0:T(8,128)S(1)}, s32[1,16]{1,0:T(1,128)S(1)}, s32[2,256]{1,0:T(2,128)S(1)}, bf16[4,4,512]{2,1,0:T(4,128)(2,1)S(1)}, bf16[4,4,512]{2,1,0:T(4,128)(2,1)S(1)}) custom-call(s32[8,16]{1,0:T(8,128)} %bitcast.11, s32[1,16]{1,0:T(1,128)} %bitcast.12, s32[2,256]{1,0:T(2,128)} %constant.8.clone.refs_2_, bf16[4,4,512]{2,1,0:T(4,128)(2,1)} %refs_3_.1, ...), custom_call_target="tpu_custom_call" | custom-call | tf_op jit(solution)/shard_map/load_blocks/pallas_call | solution.py:256
  1.5 0.0 copy-start
  1.5 0.0 copy-start.1
  1.5 0.3 %choose_blocks.1 = (bf16[256,256]{1,0:T(8,128)(2,1)S(1)}, bf16[64,256]{1,0:T(8,128)(2,1)S(1)}, bf16[128,256]{1,0:T(8,128)(2,1)S(1)}, f32[64,256]{1,0:T(8,128)S(1)}) custom-call(s32[1]{0:T(128)} %bitcast.me_ref, s32[8,16]{1,0:T(8,128)S(1)} %get-tuple-element.22.map_ref, s32[1,16]{1,0:T(1,128)S(1)} %get-tuple-element.23.count_ref, ...), custom_call_target="tpu_custom_call" | custom-call | flops 10000000000 | bytes 1000000 | tf_op jit(solution)/shard_map/choose_blocks/pallas_call | solution.py:265
  1.8 14.4 %all_to_all.10 = bf16[32,8,256]{2,1,0:T(8,128)(2,1)S(1)} all-to-all(bf16[32,8,256]{2,1,0:T(8,128)(2,1)S(1)} %bitcast.9), channel_id=1, replica_groups={{18,27,28,3,6,21,13,15,22,4,12,30,7,16,23,14,20,9,17,10,29,11,0,19,26,2..., dimensions={0} | all-to-all | bytes 262144 | tf_op jit(solution)/shard_map/all_to_all | solution.py:30
  16.2 0.0 copy-done
  16.2 0.0 copy-done.1
  16.2 2.3 %attend.1 = (bf16[256,256]{1,0:T(8,128)(2,1)S(1)}, bf16[256,2048]{1,0:T(8,128)(2,1)}, f32[16,256]{1,0:T(8,128)S(1)}, bf16[8,128,256]{2,1,0:T(8,128)(2,1)S(1)}, bf16[64,256]{1,0:T(8,128)(2,1)S(1)}) custom-call(s32[1]{0:T(128)} %bitcast.me_ref, bf16[256,2048]{1,0:T(8,128)(2,1)S(1)} %copy-done, bf16[256,2048]{1,0:T(8,128)(2,1)S(1)} %copy-done.1, ...), custom_call_target="tpu_custom_call" | custom-call | tf_op jit(solution)/shard_map/attend/pallas_call | solution.py:281
  18.5 9.0 %all_to_all.11 = bf16[32,8,256]{2,1,0:T(8,128)(2,1)S(1)} all-to-all(bf16[32,8,256]{2,1,0:T(8,128)(2,1)S(1)} %bitcast.10), channel_id=1, replica_groups={{18,27,28,3,6,21,13,15,22,4,12,30,7,16,23,14,20,9,17,10,29,11,0,19,26,2..., dimensions={0} | all-to-all | bytes 262144 | tf_op jit(solution)/shard_map/all_to_all | solution.py:30
  27.5 0.9 %sum_blocks.1 = (bf16[4,4,512]{2,1,0:T(4,128)(2,1)}, bf16[4,4,512]{2,1,0:T(4,128)(2,1)}, f32[16,256]{1,0:T(8,128)}, bf16[256,2048]{1,0:T(8,128)(2,1)}) custom-call(s32[1]{0:T(128)} %bitcast.me_ref, bf16[64,256]{1,0:T(8,128)(2,1)S(1)} %get-tuple-element.27.pick_ref, bf16[256,256]{1,0:T(8,128)(2,1)S(1)} %bitcast.8, ...), custom_call_target="tpu_custom_call", output_to_operand_aliasing={{3}: (6, {})} | custom-call | tf_op jit(solution)/shard_map/sum_blocks/pallas_call | solution.py:301
Async XLA Ops:
  1.5 14.7 %copy-start = (bf16[256,2048]{1,0:T(8,128)(2,1)S(1)}, bf16[256,2048]{1,0:T(8,128)(2,1)}, u32[]{:S(2)}) copy-start(bf16[256,2048]{1,0:T(8,128)(2,1)} %refs_0_.1) | copy-start | bytes 3145732
  1.5 14.7 %copy-start.1 = (bf16[256,2048]{1,0:T(8,128)(2,1)S(1)}, bf16[256,2048]{1,0:T(8,128)(2,1)}, u32[]{:S(2)}) copy-start(bf16[256,2048]{1,0:T(8,128)(2,1)} %refs_1_.1) | copy-start | bytes 3145732

commit v9 on v8

--- a/solution.py
+++ b/solution.py
@@ -175,9 +175,9 @@
         against_values(pair)
     for pair in range(pairs):
         soften(pair)
+        add_values(pair)
     for pair in range(pairs):
         grad_score(pair)
-        add_values(pair)
     for pair in range(pairs):
         add_queries(pair)
     for pair in range(pairs):
@@ -252,14 +252,15 @@
     params = pltpu.CompilerParams(vmem_limit_bytes=24 * 1024 * 1024)
     stay = functools.partial(pltpu.with_memory_space_constraint, memory_space=pltpu.HBM)
 
-    inputs = (block_map.T, block_count.reshape(1, spans), places, keys, values)
+    inputs = (block_map.T, block_count.reshape(1, spans), places)
     inputs = pl.pallas_call(
         load_kernel,
         out_shape=tuple(shape(part.shape, part.dtype) for part in inputs),
-        in_specs=[HBM] * 5,
-        out_specs=(VMEM,) * 5,
-        scratch_shapes=[pltpu.SemaphoreType.DMA((5,))],
+        in_specs=[HBM] * 3,
+        out_specs=(VMEM,) * 3,
+        scratch_shapes=[pltpu.SemaphoreType.DMA((3,))],
         compiler_params=params,
+        cost_estimate=pl.CostEstimate(flops=10**9, bytes_accessed=10**6, transcendentals=0),
         name="load_blocks",
     )(*map(stay, inputs))
     sent, pick, order, live = pl.pallas_call(
@@ -275,7 +276,7 @@
         compiler_params=params,
         cost_estimate=pl.CostEstimate(flops=10**10, bytes_accessed=10**6, transcendentals=0),
         name="choose_blocks",
-    )(me, *inputs)
+    )(me, *inputs, keys, values)
     got = exchange(sent.reshape(cores * spans, 2 * rows, width), order_of)
     pair_shape = (heads // 2, 2 * attended, tokens)
     terms, grad_queries, logs, gs, k = pl.pallas_call(

time: 28.7 us -> 28.6 us (level)
  no operation moved by 1% of the time
where the time goes in v9:
time: 28.6 us; the launch traced here: 28.3 us
  blocking collectives  23.3 us (81%)
  Pallas kernels  4.26 us (15%)
  between operations  0.71 us (2%)
    all_to_all x2, blocking collectives, exchange(): lax.all_to_all(parts, ('seq', 'vis'), split_axis=0, concat_axis=0, tiled=...  23.3 us
    pallas_call x1, Pallas kernels, local(): pl.pallas_call(attend_kernel, out_shape=(shape((travelling, width), BF16)...  2.3 us
    pallas_call x1, Pallas kernels, local(): pl.pallas_call(functools.partial(sum_kernel, starts), out_shape=(shape(ke...  0.87 us
    pallas_call x1, Pallas kernels, local(): pl.pallas_call(load_kernel, out_shape=tuple((shape(part.shape, part.dtype...  0.75 us

profile of v9, /device:TPU:0, one launch (start us, length us, event | category | flops | bytes accessed | tf_op | source)
XLA Modules:
  0.0 28.3 jit_solution(2082958126421265205)
XLA Ops:
  0.6 0.0 copy-start.2
  0.6 0.0 copy-start.3
  0.7 0.8 %load_blocks.1 = (s32[8,16]{1,0:T(8,128)S(1)}, s32[1,16]{1,0:T(1,128)S(1)}, s32[2,256]{1,0:T(2,128)S(1)}) custom-call(s32[8,16]{1,0:T(8,128)} %bitcast.11, s32[1,16]{1,0:T(1,128)} %bitcast.12, s32[2,256]{1,0:T(2,128)} %constant.8.clone.refs_2_), custom_call_target="tpu_custom_call" | custom-call | flops 1000000000 | bytes 1000000 | tf_op jit(solution)/shard_map/load_blocks/pallas_call | solution.py:256
  1.4 0.0 copy-done.2
  1.4 0.0 copy-done.3
  1.4 0.0 copy-start
  1.4 0.0 copy-start.1
  1.5 0.3 %choose_blocks.1 = (bf16[256,256]{1,0:T(8,128)(2,1)S(1)}, bf16[64,256]{1,0:T(8,128)(2,1)S(1)}, bf16[128,256]{1,0:T(8,128)(2,1)S(1)}, f32[64,256]{1,0:T(8,128)S(1)}) custom-call(s32[1]{0:T(128)} %bitcast.me_ref, s32[8,16]{1,0:T(8,128)S(1)} %get-tuple-element.20.map_ref, s32[1,16]{1,0:T(1,128)S(1)} %get-tuple-element.21.count_ref, ...), custom_call_target="tpu_custom_call" | custom-call | flops 10000000000 | bytes 1000000 | tf_op jit(solution)/shard_map/choose_blocks/pallas_call | solution.py:266
  1.8 14.4 %all_to_all.10 = bf16[32,8,256]{2,1,0:T(8,128)(2,1)S(1)} all-to-all(bf16[32,8,256]{2,1,0:T(8,128)(2,1)S(1)} %bitcast.10), channel_id=1, replica_groups={{18,27,28,3,6,21,13,15,22,4,12,30,7,16,23,14,20,9,17,10,29,11,0,19,26,2..., dimensions={0} | all-to-all | bytes 262144 | tf_op jit(solution)/shard_map/all_to_all | solution.py:30
  16.2 0.0 copy-done
  16.2 0.0 copy-done.1
  16.2 2.3 %attend.1 = (bf16[256,256]{1,0:T(8,128)(2,1)S(1)}, bf16[256,2048]{1,0:T(8,128)(2,1)}, f32[16,256]{1,0:T(8,128)S(1)}, bf16[8,128,256]{2,1,0:T(8,128)(2,1)S(1)}, bf16[64,256]{1,0:T(8,128)(2,1)S(1)}) custom-call(s32[1]{0:T(128)} %bitcast.me_ref, bf16[256,2048]{1,0:T(8,128)(2,1)S(1)} %copy-done, bf16[256,2048]{1,0:T(8,128)(2,1)S(1)} %copy-done.1, ...), custom_call_target="tpu_custom_call" | custom-call | tf_op jit(solution)/shard_map/attend/pallas_call | solution.py:282
  18.5 9.0 %all_to_all.11 = bf16[32,8,256]{2,1,0:T(8,128)(2,1)S(1)} all-to-all(bf16[32,8,256]{2,1,0:T(8,128)(2,1)S(1)} %bitcast.9), channel_id=1, replica_groups={{18,27,28,3,6,21,13,15,22,4,12,30,7,16,23,14,20,9,17,10,29,11,0,19,26,2..., dimensions={0} | all-to-all | bytes 262144 | tf_op jit(solution)/shard_map/all_to_all | solution.py:30
  27.5 0.9 %sum_blocks.1 = (bf16[4,4,512]{2,1,0:T(4,128)(2,1)}, bf16[4,4,512]{2,1,0:T(4,128)(2,1)}, f32[16,256]{1,0:T(8,128)}, bf16[256,2048]{1,0:T(8,128)(2,1)}) custom-call(s32[1]{0:T(128)} %bitcast.me_ref, bf16[64,256]{1,0:T(8,128)(2,1)S(1)} %get-tuple-element.23.pick_ref, bf16[256,256]{1,0:T(8,128)(2,1)S(1)} %bitcast.8, ...), custom_call_target="tpu_custom_call", output_to_operand_aliasing={{3}: (6, {})} | custom-call | tf_op jit(solution)/shard_map/sum_blocks/pallas_call | solution.py:302
Async XLA Ops:
  0.6 0.8 %copy-start.2 = (bf16[4,4,512]{2,1,0:T(4,128)(2,1)S(1)}, bf16[4,4,512]{2,1,0:T(4,128)(2,1)}, u32[]{:S(2)}) copy-start(bf16[4,4,512]{2,1,0:T(4,128)(2,1)} %keys_ref.1) | copy-start | bytes 49156
  0.6 0.8 %copy-start.3 = (bf16[4,4,512]{2,1,0:T(4,128)(2,1)S(1)}, bf16[4,4,512]{2,1,0:T(4,128)(2,1)}, u32[]{:S(2)}) copy-start(bf16[4,4,512]{2,1,0:T(4,128)(2,1)} %values_ref.1) | copy-start | bytes 49156
  1.4 14.7 %copy-start = (bf16[256,2048]{1,0:T(8,128)(2,1)S(1)}, bf16[256,2048]{1,0:T(8,128)(2,1)}, u32[]{:S(2)}) copy-start(bf16[256,2048]{1,0:T(8,128)(2,1)} %refs_0_.1) | copy-start | bytes 3145732
  1.4 14.7 %copy-start.1 = (bf16[256,2048]{1,0:T(8,128)(2,1)S(1)}, bf16[256,2048]{1,0:T(8,128)(2,1)}, u32[]{:S(2)}) copy-start(bf16[256,2048]{1,0:T(8,128)(2,1)} %refs_1_.1) | copy-start | bytes 3145732

commit v10 on v9

--- a/solution.py
+++ b/solution.py
@@ -175,13 +175,16 @@
         against_values(pair)
     for pair in range(pairs):
         soften(pair)
-        add_values(pair)
+        if not early:
+            add_values(pair)
     for pair in range(pairs):
         grad_score(pair)
     for pair in range(pairs):
         add_queries(pair)
     for pair in range(pairs):
         add_keys(pair)
+        if early:
+            add_values(pair)
     gk = [(part[:keys, :HEAD_DIM] + part[keys:, HEAD_DIM:]) * score_scale for part in gk]
     gv = [part[:keys, :HEAD_DIM] + part[keys:, HEAD_DIM:] for part in gv]
     terms = jnp.concatenate([jnp.concatenate(gk, 1), jnp.concatenate(gv, 1)], 0).astype(BF16)

time: 28.6 us -> 28.6 us (level)
  blocking collectives: 23.3 us -> 23.6 us
where the time goes in v10:
time: 28.6 us; the launch traced here: 28.3 us
  blocking collectives  23.6 us (83%)
  Pallas kernels  4.03 us (14%)
  between operations  0.71 us (2%)
    all_to_all x2, blocking collectives, exchange(): lax.all_to_all(parts, ('seq', 'vis'), split_axis=0, concat_axis=0, tiled=...  23.6 us
    pallas_call x1, Pallas kernels, local(): pl.pallas_call(attend_kernel, out_shape=(shape((travelling, width), BF16)...  2.07 us
    pallas_call x1, Pallas kernels, local(): pl.pallas_call(functools.partial(sum_kernel, starts), out_shape=(shape(ke...  0.87 us
    pallas_call x1, Pallas kernels, local(): pl.pallas_call(load_kernel, out_shape=tuple((shape(part.shape, part.dtype...  0.75 us

profile of v10, /device:TPU:0, one launch (start us, length us, event | category | flops | bytes accessed | tf_op | source)
XLA Modules:
  0.0 28.3 jit_solution(2662756969387454600)
XLA Ops:
  0.6 0.0 copy-start.2
  0.6 0.0 copy-start.3
  0.7 0.8 %load_blocks.1 = (s32[8,16]{1,0:T(8,128)S(1)}, s32[1,16]{1,0:T(1,128)S(1)}, s32[2,256]{1,0:T(2,128)S(1)}) custom-call(s32[8,16]{1,0:T(8,128)} %bitcast.11, s32[1,16]{1,0:T(1,128)} %bitcast.12, s32[2,256]{1,0:T(2,128)} %constant.8.clone.refs_2_), custom_call_target="tpu_custom_call" | custom-call | flops 1000000000 | bytes 1000000 | tf_op jit(solution)/shard_map/load_blocks/pallas_call | solution.py:259
  1.4 0.0 copy-done.2
  1.4 0.0 copy-done.3
  1.4 0.0 copy-start
  1.4 0.0 copy-start.1
  1.5 0.3 %choose_blocks.1 = (bf16[256,256]{1,0:T(8,128)(2,1)S(1)}, bf16[64,256]{1,0:T(8,128)(2,1)S(1)}, bf16[128,256]{1,0:T(8,128)(2,1)S(1)}, f32[64,256]{1,0:T(8,128)S(1)}) custom-call(s32[1]{0:T(128)} %bitcast.me_ref, s32[8,16]{1,0:T(8,128)S(1)} %get-tuple-element.20.map_ref, s32[1,16]{1,0:T(1,128)S(1)} %get-tuple-element.21.count_ref, ...), custom_call_target="tpu_custom_call" | custom-call | flops 10000000000 | bytes 1000000 | tf_op jit(solution)/shard_map/choose_blocks/pallas_call | solution.py:269
  1.8 14.4 %all_to_all.10 = bf16[32,8,256]{2,1,0:T(8,128)(2,1)S(1)} all-to-all(bf16[32,8,256]{2,1,0:T(8,128)(2,1)S(1)} %bitcast.10), channel_id=1, replica_groups={{18,27,28,3,6,21,13,15,22,4,12,30,7,16,23,14,20,9,17,10,29,11,0,19,26,2..., dimensions={0} | all-to-all | bytes 262144 | tf_op jit(solution)/shard_map/all_to_all | solution.py:30
  16.2 0.0 copy-done
  16.2 0.0 copy-done.1
  16.2 2.1 %attend.1 = (bf16[256,256]{1,0:T(8,128)(2,1)S(1)}, bf16[256,2048]{1,0:T(8,128)(2,1)}, f32[16,256]{1,0:T(8,128)S(1)}, bf16[8,128,256]{2,1,0:T(8,128)(2,1)S(1)}, bf16[64,256]{1,0:T(8,128)(2,1)S(1)}) custom-call(s32[1]{0:T(128)} %bitcast.me_ref, bf16[256,2048]{1,0:T(8,128)(2,1)S(1)} %copy-done, bf16[256,2048]{1,0:T(8,128)(2,1)S(1)} %copy-done.1, ...), custom_call_target="tpu_custom_call" | custom-call | tf_op jit(solution)/shard_map/attend/pallas_call | solution.py:285
  18.3 9.2 %all_to_all.11 = bf16[32,8,256]{2,1,0:T(8,128)(2,1)S(1)} all-to-all(bf16[32,8,256]{2,1,0:T(8,128)(2,1)S(1)} %bitcast.9), channel_id=1, replica_groups={{18,27,28,3,6,21,13,15,22,4,12,30,7,16,23,14,20,9,17,10,29,11,0,19,26,2..., dimensions={0} | all-to-all | bytes 262144 | tf_op jit(solution)/shard_map/all_to_all | solution.py:30
  27.5 0.9 %sum_blocks.1 = (bf16[4,4,512]{2,1,0:T(4,128)(2,1)}, bf16[4,4,512]{2,1,0:T(4,128)(2,1)}, f32[16,256]{1,0:T(8,128)}, bf16[256,2048]{1,0:T(8,128)(2,1)}) custom-call(s32[1]{0:T(128)} %bitcast.me_ref, bf16[64,256]{1,0:T(8,128)(2,1)S(1)} %get-tuple-element.23.pick_ref, bf16[256,256]{1,0:T(8,128)(2,1)S(1)} %bitcast.8, ...), custom_call_target="tpu_custom_call", output_to_operand_aliasing={{3}: (6, {})} | custom-call | tf_op jit(solution)/shard_map/sum_blocks/pallas_call | solution.py:305
Async XLA Ops:
  0.6 0.8 %copy-start.2 = (bf16[4,4,512]{2,1,0:T(4,128)(2,1)S(1)}, bf16[4,4,512]{2,1,0:T(4,128)(2,1)}, u32[]{:S(2)}) copy-start(bf16[4,4,512]{2,1,0:T(4,128)(2,1)} %keys_ref.1) | copy-start | bytes 49156
  0.6 0.8 %copy-start.3 = (bf16[4,4,512]{2,1,0:T(4,128)(2,1)S(1)}, bf16[4,4,512]{2,1,0:T(4,128)(2,1)}, u32[]{:S(2)}) copy-start(bf16[4,4,512]{2,1,0:T(4,128)(2,1)} %values_ref.1) | copy-start | bytes 49156
  1.4 14.7 %copy-start = (bf16[256,2048]{1,0:T(8,128)(2,1)S(1)}, bf16[256,2048]{1,0:T(8,128)(2,1)}, u32[]{:S(2)}) copy-start(bf16[256,2048]{1,0:T(8,128)(2,1)} %refs_0_.1) | copy-start | bytes 3145732
  1.4 14.7 %copy-start.1 = (bf16[256,2048]{1,0:T(8,128)(2,1)S(1)}, bf16[256,2048]{1,0:T(8,128)(2,1)}, u32[]{:S(2)}) copy-start(bf16[256,2048]{1,0:T(8,128)(2,1)} %refs_1_.1) | copy-start | bytes 3145732

commit v11 on v10

--- a/solution.py
+++ b/solution.py
@@ -18,7 +18,7 @@
 HBM = pl.BlockSpec(memory_space=pltpu.HBM)
 SMEM = pl.BlockSpec(memory_space=pltpu.SMEM)
 EXCHANGE_ORDER = {
-    (16, 2): [18, 27, 28, 3, 6, 21, 13, 15, 22, 4, 12, 30, 7, 16, 23, 14, 20, 9, 17, 10, 29, 11, 0, 19, 26, 2, 24, 5, 1, 8, 31, 25],
+    (16, 2): [21, 27, 28, 3, 29, 18, 13, 15, 22, 20, 12, 30, 7, 16, 23, 14, 4, 1, 17, 10, 6, 11, 0, 19, 26, 2, 24, 5, 9, 8, 31, 25],
 }
 
 

time: 28.6 us -> 28.6 us (level)
  no operation moved by 1% of the time
where the time goes in v11:
time: 28.6 us; the launch traced here: 28.3 us
  blocking collectives  23.6 us (83%)
  Pallas kernels  4.03 us (14%)
  between operations  0.71 us (2%)
    all_to_all x2, blocking collectives, exchange(): lax.all_to_all(parts, ('seq', 'vis'), split_axis=0, concat_axis=0, tiled=...  23.6 us
    pallas_call x1, Pallas kernels, local(): pl.pallas_call(attend_kernel, out_shape=(shape((travelling, width), BF16)...  2.07 us
    pallas_call x1, Pallas kernels, local(): pl.pallas_call(functools.partial(sum_kernel, starts), out_shape=(shape(ke...  0.87 us
    pallas_call x1, Pallas kernels, local(): pl.pallas_call(load_kernel, out_shape=tuple((shape(part.shape, part.dtype...  0.75 us

profile of v11, /device:TPU:0, one launch (start us, length us, event | category | flops | bytes accessed | tf_op | source)
XLA Modules:
  0.0 28.3 jit_solution(8370396095023609960)
XLA Ops:
  0.6 0.0 copy-start.2
  0.6 0.0 copy-start.3
  0.7 0.8 %load_blocks.1 = (s32[8,16]{1,0:T(8,128)S(1)}, s32[1,16]{1,0:T(1,128)S(1)}, s32[2,256]{1,0:T(2,128)S(1)}) custom-call(s32[8,16]{1,0:T(8,128)} %bitcast.11, s32[1,16]{1,0:T(1,128)} %bitcast.12, s32[2,256]{1,0:T(2,128)} %constant.8.clone.refs_2_), custom_call_target="tpu_custom_call" | custom-call | flops 1000000000 | bytes 1000000 | tf_op jit(solution)/shard_map/load_blocks/pallas_call | solution.py:259
  1.4 0.0 copy-done.2
  1.4 0.0 copy-done.3
  1.4 0.0 copy-start
  1.4 0.0 copy-start.1
  1.5 0.3 %choose_blocks.1 = (bf16[256,256]{1,0:T(8,128)(2,1)S(1)}, bf16[64,256]{1,0:T(8,128)(2,1)S(1)}, bf16[128,256]{1,0:T(8,128)(2,1)S(1)}, f32[64,256]{1,0:T(8,128)S(1)}) custom-call(s32[1]{0:T(128)} %bitcast.me_ref, s32[8,16]{1,0:T(8,128)S(1)} %get-tuple-element.20.map_ref, s32[1,16]{1,0:T(1,128)S(1)} %get-tuple-element.21.count_ref, ...), custom_call_target="tpu_custom_call" | custom-call | flops 10000000000 | bytes 1000000 | tf_op jit(solution)/shard_map/choose_blocks/pallas_call | solution.py:269
  1.8 14.4 %all_to_all.10 = bf16[32,8,256]{2,1,0:T(8,128)(2,1)S(1)} all-to-all(bf16[32,8,256]{2,1,0:T(8,128)(2,1)S(1)} %bitcast.10), channel_id=1, replica_groups={{21,27,28,3,29,18,13,15,22,20,12,30,7,16,23,14,4,1,17,10,6,11,0,19,26,2..., dimensions={0} | all-to-all | bytes 262144 | tf_op jit(solution)/shard_map/all_to_all | solution.py:30
  16.2 0.0 copy-done
  16.2 0.0 copy-done.1
  16.2 2.1 %attend.1 = (bf16[256,256]{1,0:T(8,128)(2,1)S(1)}, bf16[256,2048]{1,0:T(8,128)(2,1)}, f32[16,256]{1,0:T(8,128)S(1)}, bf16[8,128,256]{2,1,0:T(8,128)(2,1)S(1)}, bf16[64,256]{1,0:T(8,128)(2,1)S(1)}) custom-call(s32[1]{0:T(128)} %bitcast.me_ref, bf16[256,2048]{1,0:T(8,128)(2,1)S(1)} %copy-done, bf16[256,2048]{1,0:T(8,128)(2,1)S(1)} %copy-done.1, ...), custom_call_target="tpu_custom_call" | custom-call | tf_op jit(solution)/shard_map/attend/pallas_call | solution.py:285
  18.3 9.2 %all_to_all.11 = bf16[32,8,256]{2,1,0:T(8,128)(2,1)S(1)} all-to-all(bf16[32,8,256]{2,1,0:T(8,128)(2,1)S(1)} %bitcast.9), channel_id=1, replica_groups={{21,27,28,3,29,18,13,15,22,20,12,30,7,16,23,14,4,1,17,10,6,11,0,19,26,2..., dimensions={0} | all-to-all | bytes 262144 | tf_op jit(solution)/shard_map/all_to_all | solution.py:30
  27.4 0.9 %sum_blocks.1 = (bf16[4,4,512]{2,1,0:T(4,128)(2,1)}, bf16[4,4,512]{2,1,0:T(4,128)(2,1)}, f32[16,256]{1,0:T(8,128)}, bf16[256,2048]{1,0:T(8,128)(2,1)}) custom-call(s32[1]{0:T(128)} %bitcast.me_ref, bf16[64,256]{1,0:T(8,128)(2,1)S(1)} %get-tuple-element.23.pick_ref, bf16[256,256]{1,0:T(8,128)(2,1)S(1)} %bitcast.8, ...), custom_call_target="tpu_custom_call", output_to_operand_aliasing={{3}: (6, {})} | custom-call | tf_op jit(solution)/shard_map/sum_blocks/pallas_call | solution.py:305
Async XLA Ops:
  0.6 0.8 %copy-start.2 = (bf16[4,4,512]{2,1,0:T(4,128)(2,1)S(1)}, bf16[4,4,512]{2,1,0:T(4,128)(2,1)}, u32[]{:S(2)}) copy-start(bf16[4,4,512]{2,1,0:T(4,128)(2,1)} %keys_ref.1) | copy-start | bytes 49156
  0.6 0.8 %copy-start.3 = (bf16[4,4,512]{2,1,0:T(4,128)(2,1)S(1)}, bf16[4,4,512]{2,1,0:T(4,128)(2,1)}, u32[]{:S(2)}) copy-start(bf16[4,4,512]{2,1,0:T(4,128)(2,1)} %values_ref.1) | copy-start | bytes 49156
  1.4 14.7 %copy-start = (bf16[256,2048]{1,0:T(8,128)(2,1)S(1)}, bf16[256,2048]{1,0:T(8,128)(2,1)}, u32[]{:S(2)}) copy-start(bf16[256,2048]{1,0:T(8,128)(2,1)} %refs_0_.1) | copy-start | bytes 3145732
  1.4 14.7 %copy-start.1 = (bf16[256,2048]{1,0:T(8,128)(2,1)S(1)}, bf16[256,2048]{1,0:T(8,128)(2,1)}, u32[]{:S(2)}) copy-start(bf16[256,2048]{1,0:T(8,128)(2,1)} %refs_1_.1) | copy-start | bytes 3145732
